TPU v7x, 256 devices: a whole 4x4x8 slice. The times are simulated.
256 devices in a mesh: blk: 32 (over y_lo, z, core), grp: 8 (over x, y_hi).
Axes of the slice: x: 4, y: 4 (y_hi: 2, y_lo: 2; y = y_hi * 2 + y_lo), z: 8, core: 2. Of those that a mesh axis runs over, the one named last changes fastest.
Arguments:
- queries: bfloat16 [8192, 2048], P(('blk', 'grp')), may hold values from -6 to 6
- windows: int32 [512], P(('blk', 'grp')), may hold values from 0 to 28
- library: bfloat16 [12288, 2048], P(('blk', 'grp')), may hold values from -6 to 6
- bands: int32 [1536], P(('blk', 'grp')), may hold values from 0 to 31
- shifts: int32 [4], replicated, may hold values from -24 to 24
Outputs:
- scored: float32 [8192, 16], P(('blk', 'grp'))
All inputs are finite; a program needn't handle non-finite values.
Results may differ from a plain program's by a relative error of at most 0.0003.
Values may be sent and summed in bfloat16 or wider, within the bound.
A program may use at most 128 MiB of HBM per device.

v0:
```python
import math

import jax
import jax.numpy as jnp
from jax import lax
from jax.sharding import PartitionSpec as P

BINS = 2048
NOFF = 4
TOPK = 16
MAXSHIFT = 24
QBLK = 16
LBLK = 8
SPAN = 4


EPS = 1e-06
MASKED = -8.0


def from_behind(block, axis, distance):
    devices = range(lax.axis_size(axis))
    route = [((i - distance) % len(devices), i) for i in devices]
    return lax.ppermute(block, axis, route)


def best_values(values):
    ordered = -jnp.sort(-values, axis=1)
    return ordered[:, :TOPK]


def shifted_stack(lib_rows, shifts):
    padded = jnp.pad(lib_rows, ((0, 0), (MAXSHIFT, MAXSHIFT)))
    return jnp.concatenate(
        [
            lax.dynamic_slice_in_dim(padded, MAXSHIFT - shifts[index], BINS, 1)
            for index in range(NOFF)
        ],
        axis=0,
    )


def local(queries, windows, library, bands, shifts):
    group_q, group_w = (
        lax.all_gather(queries, "grp", axis=0, tiled=True),
        lax.all_gather(windows, "grp", axis=0, tiled=True),
    )
    query_scale = lax.rsqrt(jnp.mean(jnp.square(group_q.astype(jnp.float32)), axis=1) + EPS)
    query_win = jnp.repeat(group_w, QBLK)
    row_band = jnp.repeat(bands, LBLK)
    inv_root = 1.0 / math.sqrt(BINS)
    group_rows = group_q.shape[0]

    def fold_in(best, lib_rows, lib_band):
        inside = (lib_band[None, :] >= query_win[:, None]) & (
            lib_band[None, :] < query_win[:, None] + SPAN
        )
        stacked = shifted_stack(lib_rows, shifts)
        product = lax.dot_general(
            group_q, stacked, (((1,), (1,)), ((), ())), preferred_element_type=jnp.float32
        )
        count = lib_rows.shape[0]
        top = jnp.max(product.reshape(group_rows, NOFF, count), axis=1)
        lib_wide = lib_rows.astype(jnp.float32)
        lib_scale = lax.rsqrt(jnp.mean(lib_wide * lib_wide, axis=1) + EPS)
        score = top * query_scale[:, None] * lib_scale[None, :] * inv_root
        score = jnp.where(inside, score, MASKED)
        return best_values(jnp.concatenate([best, score], axis=1))

    initial = jnp.full((group_rows, TOPK), MASKED, jnp.float32)
    length = lax.axis_size("blk")
    best = fold_in(initial, library, row_band)

    def one_step(step, state):
        current, lib_rows, lib_band = state
        lib_rows, lib_band = from_behind((lib_rows, lib_band), "blk", 1)
        return (fold_in(current, lib_rows, lib_band), lib_rows, lib_band)

    best, lib_rows, lib_band = lax.fori_loop(0, length - 1, one_step, (best, library, row_band))
    own_rows = queries.shape[0]
    pooled = lax.all_gather(best, "grp", axis=1, tiled=True)
    mine = lax.dynamic_slice_in_dim(pooled, lax.axis_index("grp") * own_rows, own_rows, 0)
    result = best_values(mine)
    return result


def solution(mesh):
    return jax.shard_map(
        local,
        mesh=mesh,
        in_specs=(
            P(("blk", "grp"), None),
            P(("blk", "grp")),
            P(("blk", "grp"), None),
            P(("blk", "grp")),
            P(),
        ),
        out_specs=P(("blk", "grp"), None),
        check_vma=False,
    )
```

profile of v0, /device:TPU:8, one launch (start us, length us, event | category | flops | bytes accessed | tf_op | source)
XLA Modules:
  0.0 438.0 jit_solution(2369161213121654100)
XLA Ops:
  17.1 13.2 %all-reduce.3 = s32[16]{0:T(128)S(1)} all-reduce(s32[16]{0:T(128)S(1)} %dynamic-update-slice), channel_id=1, replica_groups=mesh['blk'=32,'grp'=8] {'grp'}, use_global_device_ids=true, to_apply=%add.3 | all-reduce | flops 16 | bytes 128
  31.8 32.7 %all-gather.2.cloned.1.call-done = bf16[256,2048]{1,0:T(8,128)(2,1)} async-done(((bf16[32,2048]{1,0:T(8,128)(2,1)}), bf16[256,2048]{1,0:T(8,128)(2,1)}) %all-gather.2.cloned.1.call-update) | async-done | bytes 1048592 | tf_op jit(solution)/shard_map/all_gather | solution.py:45
  66.7 1.9 sort.46
  68.6 324.7 %while.18 = (s32[]{:T(128)}, f32[256,16]{0,1:T(8,128)S(1)}, bf16[48,2048]{1,0:T(8,128)(2,1)S(1)}, s32[48]{0:T(128)S(1)}, s32[]{:T(128)}, /*index=5*/s32[]{:T(128...) while((s32[]{:T(128)}, f32[256,16]{0,1:T(8,128)S(1)}, ...), condition=%wide.region_8.9_spmd.clone, body=%wide.region_4.8_spmd.clone.sunk | while | flops 205156656 | bytes 5237089 | solution.py:79
  70.4 5.4 %collective-permute-done.1 = s32[48]{0:T(128)S(1)} collective-permute-done((s32[48]{0:T(128)S(1)}, s32[48]{0:T(128)S(1)}, u32[]{:S(2)}, u32[]{:S(2)}) %collective-permute-start.1) | collective-permute-done | bytes 224 | tf_op jit(solution)/shard_map/while/body/eval_jaxpr/ppermute | solution.py:24
  77.1 1.9 sort.50
  79.4 7.0 %collective-permute-done.1 = s32[48]{0:T(128)S(1)} collective-permute-done((s32[48]{0:T(128)S(1)}, s32[48]{0:T(128)S(1)}, u32[]{:S(2)}, u32[]{:S(2)}) %collective-permute-start.1) | collective-permute-done | bytes 224 | tf_op jit(solution)/shard_map/while/body/eval_jaxpr/ppermute | solution.py:24
  87.6 1.9 sort.50
  89.8 7.0 %collective-permute-done.1 = s32[48]{0:T(128)S(1)} collective-permute-done((s32[48]{0:T(128)S(1)}, s32[48]{0:T(128)S(1)}, u32[]{:S(2)}, u32[]{:S(2)}) %collective-permute-start.1) | collective-permute-done | bytes 224 | tf_op jit(solution)/shard_map/while/body/eval_jaxpr/ppermute | solution.py:24
  98.0 1.9 sort.50
  100.3 7.0 %collective-permute-done.1 = s32[48]{0:T(128)S(1)} collective-permute-done((s32[48]{0:T(128)S(1)}, s32[48]{0:T(128)S(1)}, u32[]{:S(2)}, u32[]{:S(2)}) %collective-permute-start.1) | collective-permute-done | bytes 224 | tf_op jit(solution)/shard_map/while/body/eval_jaxpr/ppermute | solution.py:24
  108.5 1.9 sort.50
  110.8 7.0 %collective-permute-done.1 = s32[48]{0:T(128)S(1)} collective-permute-done((s32[48]{0:T(128)S(1)}, s32[48]{0:T(128)S(1)}, u32[]{:S(2)}, u32[]{:S(2)}) %collective-permute-start.1) | collective-permute-done | bytes 224 | tf_op jit(solution)/shard_map/while/body/eval_jaxpr/ppermute | solution.py:24
  119.0 1.9 sort.50
  121.3 7.0 %collective-permute-done.1 = s32[48]{0:T(128)S(1)} collective-permute-done((s32[48]{0:T(128)S(1)}, s32[48]{0:T(128)S(1)}, u32[]{:S(2)}, u32[]{:S(2)}) %collective-permute-start.1) | collective-permute-done | bytes 224 | tf_op jit(solution)/shard_map/while/body/eval_jaxpr/ppermute | solution.py:24
  129.5 1.9 sort.50
  131.7 7.0 %collective-permute-done.1 = s32[48]{0:T(128)S(1)} collective-permute-done((s32[48]{0:T(128)S(1)}, s32[48]{0:T(128)S(1)}, u32[]{:S(2)}, u32[]{:S(2)}) %collective-permute-start.1) | collective-permute-done | bytes 224 | tf_op jit(solution)/shard_map/while/body/eval_jaxpr/ppermute | solution.py:24
  140.0 1.9 sort.50
  142.2 7.0 %collective-permute-done.1 = s32[48]{0:T(128)S(1)} collective-permute-done((s32[48]{0:T(128)S(1)}, s32[48]{0:T(128)S(1)}, u32[]{:S(2)}, u32[]{:S(2)}) %collective-permute-start.1) | collective-permute-done | bytes 224 | tf_op jit(solution)/shard_map/while/body/eval_jaxpr/ppermute | solution.py:24
  150.4 1.9 sort.50
  152.7 7.0 %collective-permute-done.1 = s32[48]{0:T(128)S(1)} collective-permute-done((s32[48]{0:T(128)S(1)}, s32[48]{0:T(128)S(1)}, u32[]{:S(2)}, u32[]{:S(2)}) %collective-permute-start.1) | collective-permute-done | bytes 224 | tf_op jit(solution)/shard_map/while/body/eval_jaxpr/ppermute | solution.py:24
  160.9 1.9 sort.50
  163.2 7.0 %collective-permute-done.1 = s32[48]{0:T(128)S(1)} collective-permute-done((s32[48]{0:T(128)S(1)}, s32[48]{0:T(128)S(1)}, u32[]{:S(2)}, u32[]{:S(2)}) %collective-permute-start.1) | collective-permute-done | bytes 224 | tf_op jit(solution)/shard_map/while/body/eval_jaxpr/ppermute | solution.py:24
  171.4 1.9 sort.50
  173.6 7.0 %collective-permute-done.1 = s32[48]{0:T(128)S(1)} collective-permute-done((s32[48]{0:T(128)S(1)}, s32[48]{0:T(128)S(1)}, u32[]{:S(2)}, u32[]{:S(2)}) %collective-permute-start.1) | collective-permute-done | bytes 224 | tf_op jit(solution)/shard_map/while/body/eval_jaxpr/ppermute | solution.py:24
  181.9 1.9 sort.50
  184.1 7.0 %collective-permute-done.1 = s32[48]{0:T(128)S(1)} collective-permute-done((s32[48]{0:T(128)S(1)}, s32[48]{0:T(128)S(1)}, u32[]{:S(2)}, u32[]{:S(2)}) %collective-permute-start.1) | collective-permute-done | bytes 224 | tf_op jit(solution)/shard_map/while/body/eval_jaxpr/ppermute | solution.py:24
  192.3 1.9 sort.50
  194.6 7.0 %collective-permute-done.1 = s32[48]{0:T(128)S(1)} collective-permute-done((s32[48]{0:T(128)S(1)}, s32[48]{0:T(128)S(1)}, u32[]{:S(2)}, u32[]{:S(2)}) %collective-permute-start.1) | collective-permute-done | bytes 224 | tf_op jit(solution)/shard_map/while/body/eval_jaxpr/ppermute | solution.py:24
  202.8 1.9 sort.50
  205.1 7.0 %collective-permute-done.1 = s32[48]{0:T(128)S(1)} collective-permute-done((s32[48]{0:T(128)S(1)}, s32[48]{0:T(128)S(1)}, u32[]{:S(2)}, u32[]{:S(2)}) %collective-permute-start.1) | collective-permute-done | bytes 224 | tf_op jit(solution)/shard_map/while/body/eval_jaxpr/ppermute | solution.py:24
  213.3 1.9 sort.50
  215.5 7.0 %collective-permute-done.1 = s32[48]{0:T(128)S(1)} collective-permute-done((s32[48]{0:T(128)S(1)}, s32[48]{0:T(128)S(1)}, u32[]{:S(2)}, u32[]{:S(2)}) %collective-permute-start.1) | collective-permute-done | bytes 224 | tf_op jit(solution)/shard_map/while/body/eval_jaxpr/ppermute | solution.py:24
  223.8 1.9 sort.50
  226.0 7.0 %collective-permute-done.1 = s32[48]{0:T(128)S(1)} collective-permute-done((s32[48]{0:T(128)S(1)}, s32[48]{0:T(128)S(1)}, u32[]{:S(2)}, u32[]{:S(2)}) %collective-permute-start.1) | collective-permute-done | bytes 224 | tf_op jit(solution)/shard_map/while/body/eval_jaxpr/ppermute | solution.py:24
  234.2 1.9 sort.50
  236.5 7.0 %collective-permute-done.1 = s32[48]{0:T(128)S(1)} collective-permute-done((s32[48]{0:T(128)S(1)}, s32[48]{0:T(128)S(1)}, u32[]{:S(2)}, u32[]{:S(2)}) %collective-permute-start.1) | collective-permute-done | bytes 224 | tf_op jit(solution)/shard_map/while/body/eval_jaxpr/ppermute | solution.py:24
  244.7 1.9 sort.50
  247.0 7.0 %collective-permute-done.1 = s32[48]{0:T(128)S(1)} collective-permute-done((s32[48]{0:T(128)S(1)}, s32[48]{0:T(128)S(1)}, u32[]{:S(2)}, u32[]{:S(2)}) %collective-permute-start.1) | collective-permute-done | bytes 224 | tf_op jit(solution)/shard_map/while/body/eval_jaxpr/ppermute | solution.py:24
  255.2 1.9 sort.50
  257.5 7.0 %collective-permute-done.1 = s32[48]{0:T(128)S(1)} collective-permute-done((s32[48]{0:T(128)S(1)}, s32[48]{0:T(128)S(1)}, u32[]{:S(2)}, u32[]{:S(2)}) %collective-permute-start.1) | collective-permute-done | bytes 224 | tf_op jit(solution)/shard_map/while/body/eval_jaxpr/ppermute | solution.py:24
  265.7 1.9 sort.50
  267.9 7.0 %collective-permute-done.1 = s32[48]{0:T(128)S(1)} collective-permute-done((s32[48]{0:T(128)S(1)}, s32[48]{0:T(128)S(1)}, u32[]{:S(2)}, u32[]{:S(2)}) %collective-permute-start.1) | collective-permute-done | bytes 224 | tf_op jit(solution)/shard_map/while/body/eval_jaxpr/ppermute | solution.py:24
  278.4 7.0 %collective-permute-done.1 = s32[48]{0:T(128)S(1)} collective-permute-done((s32[48]{0:T(128)S(1)}, s32[48]{0:T(128)S(1)}, u32[]{:S(2)}, u32[]{:S(2)}) %collective-permute-start.1) | collective-permute-done | bytes 224 | tf_op jit(solution)/shard_map/while/body/eval_jaxpr/ppermute | solution.py:24
  286.6 1.9 sort.50
  288.9 7.0 %collective-permute-done.1 = s32[48]{0:T(128)S(1)} collective-permute-done((s32[48]{0:T(128)S(1)}, s32[48]{0:T(128)S(1)}, u32[]{:S(2)}, u32[]{:S(2)}) %collective-permute-start.1) | collective-permute-done | bytes 224 | tf_op jit(solution)/shard_map/while/body/eval_jaxpr/ppermute | solution.py:24
  299.4 7.0 %collective-permute-done.1 = s32[48]{0:T(128)S(1)} collective-permute-done((s32[48]{0:T(128)S(1)}, s32[48]{0:T(128)S(1)}, u32[]{:S(2)}, u32[]{:S(2)}) %collective-permute-start.1) | collective-permute-done | bytes 224 | tf_op jit(solution)/shard_map/while/body/eval_jaxpr/ppermute | solution.py:24
  307.6 1.9 sort.50
  309.8 7.0 %collective-permute-done.1 = s32[48]{0:T(128)S(1)} collective-permute-done((s32[48]{0:T(128)S(1)}, s32[48]{0:T(128)S(1)}, u32[]{:S(2)}, u32[]{:S(2)}) %collective-permute-start.1) | collective-permute-done | bytes 224 | tf_op jit(solution)/shard_map/while/body/eval_jaxpr/ppermute | solution.py:24
  320.3 7.0 %collective-permute-done.1 = s32[48]{0:T(128)S(1)} collective-permute-done((s32[48]{0:T(128)S(1)}, s32[48]{0:T(128)S(1)}, u32[]{:S(2)}, u32[]{:S(2)}) %collective-permute-start.1) | collective-permute-done | bytes 224 | tf_op jit(solution)/shard_map/while/body/eval_jaxpr/ppermute | solution.py:24
  328.5 1.9 sort.50
  330.8 7.0 %collective-permute-done.1 = s32[48]{0:T(128)S(1)} collective-permute-done((s32[48]{0:T(128)S(1)}, s32[48]{0:T(128)S(1)}, u32[]{:S(2)}, u32[]{:S(2)}) %collective-permute-start.1) | collective-permute-done | bytes 224 | tf_op jit(solution)/shard_map/while/body/eval_jaxpr/ppermute | solution.py:24
  341.3 7.0 %collective-permute-done.1 = s32[48]{0:T(128)S(1)} collective-permute-done((s32[48]{0:T(128)S(1)}, s32[48]{0:T(128)S(1)}, u32[]{:S(2)}, u32[]{:S(2)}) %collective-permute-start.1) | collective-permute-done | bytes 224 | tf_op jit(solution)/shard_map/while/body/eval_jaxpr/ppermute | solution.py:24
  349.5 1.9 sort.50
  351.7 7.0 %collective-permute-done.1 = s32[48]{0:T(128)S(1)} collective-permute-done((s32[48]{0:T(128)S(1)}, s32[48]{0:T(128)S(1)}, u32[]{:S(2)}, u32[]{:S(2)}) %collective-permute-start.1) | collective-permute-done | bytes 224 | tf_op jit(solution)/shard_map/while/body/eval_jaxpr/ppermute | solution.py:24
  359.9 1.9 sort.50
  362.2 7.0 %collective-permute-done.1 = s32[48]{0:T(128)S(1)} collective-permute-done((s32[48]{0:T(128)S(1)}, s32[48]{0:T(128)S(1)}, u32[]{:S(2)}, u32[]{:S(2)}) %collective-permute-start.1) | collective-permute-done | bytes 224 | tf_op jit(solution)/shard_map/while/body/eval_jaxpr/ppermute | solution.py:24
  370.4 1.9 sort.50
  372.7 7.0 %collective-permute-done.1 = s32[48]{0:T(128)S(1)} collective-permute-done((s32[48]{0:T(128)S(1)}, s32[48]{0:T(128)S(1)}, u32[]{:S(2)}, u32[]{:S(2)}) %collective-permute-start.1) | collective-permute-done | bytes 224 | tf_op jit(solution)/shard_map/while/body/eval_jaxpr/ppermute | solution.py:24
  380.9 1.9 sort.50
  383.2 7.0 %collective-permute-done.1 = s32[48]{0:T(128)S(1)} collective-permute-done((s32[48]{0:T(128)S(1)}, s32[48]{0:T(128)S(1)}, u32[]{:S(2)}, u32[]{:S(2)}) %collective-permute-start.1) | collective-permute-done | bytes 224 | tf_op jit(solution)/shard_map/while/body/eval_jaxpr/ppermute | solution.py:24
  391.4 1.9 sort.50
  393.3 34.2 %all_gather.11 = f32[256,128]{0,1:T(8,128)S(1)} all-gather(f32[256,16]{0,1:T(8,128)S(1)} %get-tuple-element.201), channel_id=1, replica_groups=mesh['blk'=32,'grp'=8] {'grp'}, dimensions={1}, use_global_device_ids=true | all-gather | bytes 147456 | tf_op jit(solution)/shard_map/all_gather | solution.py:81
  427.7 2.9 sort.47
  (562 shorter events, 65.0 us)
Async XLA Ops:
  6.5 57.9 %all-gather.2.cloned.1.call-start = ((), (), s32[]{:S(2)}) async-start(), calls=%async_computation | async-start | bytes 1179648 | tf_op jit(solution)/shard_map/all_gather | solution.py:45
  64.5 1.6 copy-start
  68.6 7.3 %collective-permute-start = (bf16[48,2048]{1,0:T(8,128)(2,1)S(1)}, bf16[48,2048]{1,0:T(8,128)(2,1)S(1)}, u32[]{:S(2)}, u32[]{:S(2)}) collective-permute-start(bf16[48,2048]{1,0:T(8,128)(2,1)S(1)} %get-tuple-element.355), channel_id=1, source_target_pairs={{248,0},{0,8},{8,16},{16,24},{24,32},{32,40},{40,48},{48,56},{56,6... | collective-permute-start | bytes 589832 | tf_op jit(solution)/shard_map/while/body/eval_jaxpr/ppermute | solution.py:24
  68.6 7.3 %collective-permute-start.1 = (s32[48]{0:T(128)S(1)}, s32[48]{0:T(128)S(1)}, u32[]{:S(2)}, u32[]{:S(2)}) collective-permute-start(s32[48]{0:T(128)S(1)} %get-tuple-element.356), channel_id=1, source_target_pairs={{248,0},{0,8},{8,16},{16,24},{24,32},{32,40},{40,48},{48,56},{56,6... | collective-permute-start | bytes 584 | tf_op jit(solution)/shard_map/while/body/eval_jaxpr/ppermute | solution.py:24
  79.0 7.3 %collective-permute-start = (bf16[48,2048]{1,0:T(8,128)(2,1)S(1)}, bf16[48,2048]{1,0:T(8,128)(2,1)S(1)}, u32[]{:S(2)}, u32[]{:S(2)}) collective-permute-start(bf16[48,2048]{1,0:T(8,128)(2,1)S(1)} %get-tuple-element.355), channel_id=1, source_target_pairs={{248,0},{0,8},{8,16},{16,24},{24,32},{32,40},{40,48},{48,56},{56,6... | collective-permute-start | bytes 589832 | tf_op jit(solution)/shard_map/while/body/eval_jaxpr/ppermute | solution.py:24
  79.1 7.3 %collective-permute-start.1 = (s32[48]{0:T(128)S(1)}, s32[48]{0:T(128)S(1)}, u32[]{:S(2)}, u32[]{:S(2)}) collective-permute-start(s32[48]{0:T(128)S(1)} %get-tuple-element.356), channel_id=1, source_target_pairs={{248,0},{0,8},{8,16},{16,24},{24,32},{32,40},{40,48},{48,56},{56,6... | collective-permute-start | bytes 584 | tf_op jit(solution)/shard_map/while/body/eval_jaxpr/ppermute | solution.py:24
  89.5 7.3 %collective-permute-start = (bf16[48,2048]{1,0:T(8,128)(2,1)S(1)}, bf16[48,2048]{1,0:T(8,128)(2,1)S(1)}, u32[]{:S(2)}, u32[]{:S(2)}) collective-permute-start(bf16[48,2048]{1,0:T(8,128)(2,1)S(1)} %get-tuple-element.355), channel_id=1, source_target_pairs={{248,0},{0,8},{8,16},{16,24},{24,32},{32,40},{40,48},{48,56},{56,6... | collective-permute-start | bytes 589832 | tf_op jit(solution)/shard_map/while/body/eval_jaxpr/ppermute | solution.py:24
  89.6 7.3 %collective-permute-start.1 = (s32[48]{0:T(128)S(1)}, s32[48]{0:T(128)S(1)}, u32[]{:S(2)}, u32[]{:S(2)}) collective-permute-start(s32[48]{0:T(128)S(1)} %get-tuple-element.356), channel_id=1, source_target_pairs={{248,0},{0,8},{8,16},{16,24},{24,32},{32,40},{40,48},{48,56},{56,6... | collective-permute-start | bytes 584 | tf_op jit(solution)/shard_map/while/body/eval_jaxpr/ppermute | solution.py:24
  100.0 7.3 %collective-permute-start = (bf16[48,2048]{1,0:T(8,128)(2,1)S(1)}, bf16[48,2048]{1,0:T(8,128)(2,1)S(1)}, u32[]{:S(2)}, u32[]{:S(2)}) collective-permute-start(bf16[48,2048]{1,0:T(8,128)(2,1)S(1)} %get-tuple-element.355), channel_id=1, source_target_pairs={{248,0},{0,8},{8,16},{16,24},{24,32},{32,40},{40,48},{48,56},{56,6... | collective-permute-start | bytes 589832 | tf_op jit(solution)/shard_map/while/body/eval_jaxpr/ppermute | solution.py:24
  100.1 7.3 %collective-permute-start.1 = (s32[48]{0:T(128)S(1)}, s32[48]{0:T(128)S(1)}, u32[]{:S(2)}, u32[]{:S(2)}) collective-permute-start(s32[48]{0:T(128)S(1)} %get-tuple-element.356), channel_id=1, source_target_pairs={{248,0},{0,8},{8,16},{16,24},{24,32},{32,40},{40,48},{48,56},{56,6... | collective-permute-start | bytes 584 | tf_op jit(solution)/shard_map/while/body/eval_jaxpr/ppermute | solution.py:24
  110.4 7.3 %collective-permute-start = (bf16[48,2048]{1,0:T(8,128)(2,1)S(1)}, bf16[48,2048]{1,0:T(8,128)(2,1)S(1)}, u32[]{:S(2)}, u32[]{:S(2)}) collective-permute-start(bf16[48,2048]{1,0:T(8,128)(2,1)S(1)} %get-tuple-element.355), channel_id=1, source_target_pairs={{248,0},{0,8},{8,16},{16,24},{24,32},{32,40},{40,48},{48,56},{56,6... | collective-permute-start | bytes 589832 | tf_op jit(solution)/shard_map/while/body/eval_jaxpr/ppermute | solution.py:24
  110.5 7.3 %collective-permute-start.1 = (s32[48]{0:T(128)S(1)}, s32[48]{0:T(128)S(1)}, u32[]{:S(2)}, u32[]{:S(2)}) collective-permute-start(s32[48]{0:T(128)S(1)} %get-tuple-element.356), channel_id=1, source_target_pairs={{248,0},{0,8},{8,16},{16,24},{24,32},{32,40},{40,48},{48,56},{56,6... | collective-permute-start | bytes 584 | tf_op jit(solution)/shard_map/while/body/eval_jaxpr/ppermute | solution.py:24
  120.9 7.3 %collective-permute-start = (bf16[48,2048]{1,0:T(8,128)(2,1)S(1)}, bf16[48,2048]{1,0:T(8,128)(2,1)S(1)}, u32[]{:S(2)}, u32[]{:S(2)}) collective-permute-start(bf16[48,2048]{1,0:T(8,128)(2,1)S(1)} %get-tuple-element.355), channel_id=1, source_target_pairs={{248,0},{0,8},{8,16},{16,24},{24,32},{32,40},{40,48},{48,56},{56,6... | collective-permute-start | bytes 589832 | tf_op jit(solution)/shard_map/while/body/eval_jaxpr/ppermute | solution.py:24
  121.0 7.3 %collective-permute-start.1 = (s32[48]{0:T(128)S(1)}, s32[48]{0:T(128)S(1)}, u32[]{:S(2)}, u32[]{:S(2)}) collective-permute-start(s32[48]{0:T(128)S(1)} %get-tuple-element.356), channel_id=1, source_target_pairs={{248,0},{0,8},{8,16},{16,24},{24,32},{32,40},{40,48},{48,56},{56,6... | collective-permute-start | bytes 584 | tf_op jit(solution)/shard_map/while/body/eval_jaxpr/ppermute | solution.py:24
  131.4 7.3 %collective-permute-start = (bf16[48,2048]{1,0:T(8,128)(2,1)S(1)}, bf16[48,2048]{1,0:T(8,128)(2,1)S(1)}, u32[]{:S(2)}, u32[]{:S(2)}) collective-permute-start(bf16[48,2048]{1,0:T(8,128)(2,1)S(1)} %get-tuple-element.355), channel_id=1, source_target_pairs={{248,0},{0,8},{8,16},{16,24},{24,32},{32,40},{40,48},{48,56},{56,6... | collective-permute-start | bytes 589832 | tf_op jit(solution)/shard_map/while/body/eval_jaxpr/ppermute | solution.py:24
  131.5 7.3 %collective-permute-start.1 = (s32[48]{0:T(128)S(1)}, s32[48]{0:T(128)S(1)}, u32[]{:S(2)}, u32[]{:S(2)}) collective-permute-start(s32[48]{0:T(128)S(1)} %get-tuple-element.356), channel_id=1, source_target_pairs={{248,0},{0,8},{8,16},{16,24},{24,32},{32,40},{40,48},{48,56},{56,6... | collective-permute-start | bytes 584 | tf_op jit(solution)/shard_map/while/body/eval_jaxpr/ppermute | solution.py:24
  141.9 7.3 %collective-permute-start = (bf16[48,2048]{1,0:T(8,128)(2,1)S(1)}, bf16[48,2048]{1,0:T(8,128)(2,1)S(1)}, u32[]{:S(2)}, u32[]{:S(2)}) collective-permute-start(bf16[48,2048]{1,0:T(8,128)(2,1)S(1)} %get-tuple-element.355), channel_id=1, source_target_pairs={{248,0},{0,8},{8,16},{16,24},{24,32},{32,40},{40,48},{48,56},{56,6... | collective-permute-start | bytes 589832 | tf_op jit(solution)/shard_map/while/body/eval_jaxpr/ppermute | solution.py:24
  142.0 7.3 %collective-permute-start.1 = (s32[48]{0:T(128)S(1)}, s32[48]{0:T(128)S(1)}, u32[]{:S(2)}, u32[]{:S(2)}) collective-permute-start(s32[48]{0:T(128)S(1)} %get-tuple-element.356), channel_id=1, source_target_pairs={{248,0},{0,8},{8,16},{16,24},{24,32},{32,40},{40,48},{48,56},{56,6... | collective-permute-start | bytes 584 | tf_op jit(solution)/shard_map/while/body/eval_jaxpr/ppermute | solution.py:24
  152.3 7.3 %collective-permute-start = (bf16[48,2048]{1,0:T(8,128)(2,1)S(1)}, bf16[48,2048]{1,0:T(8,128)(2,1)S(1)}, u32[]{:S(2)}, u32[]{:S(2)}) collective-permute-start(bf16[48,2048]{1,0:T(8,128)(2,1)S(1)} %get-tuple-element.355), channel_id=1, source_target_pairs={{248,0},{0,8},{8,16},{16,24},{24,32},{32,40},{40,48},{48,56},{56,6... | collective-permute-start | bytes 589832 | tf_op jit(solution)/shard_map/while/body/eval_jaxpr/ppermute | solution.py:24
  152.4 7.3 %collective-permute-start.1 = (s32[48]{0:T(128)S(1)}, s32[48]{0:T(128)S(1)}, u32[]{:S(2)}, u32[]{:S(2)}) collective-permute-start(s32[48]{0:T(128)S(1)} %get-tuple-element.356), channel_id=1, source_target_pairs={{248,0},{0,8},{8,16},{16,24},{24,32},{32,40},{40,48},{48,56},{56,6... | collective-permute-start | bytes 584 | tf_op jit(solution)/shard_map/while/body/eval_jaxpr/ppermute | solution.py:24
  162.8 7.3 %collective-permute-start = (bf16[48,2048]{1,0:T(8,128)(2,1)S(1)}, bf16[48,2048]{1,0:T(8,128)(2,1)S(1)}, u32[]{:S(2)}, u32[]{:S(2)}) collective-permute-start(bf16[48,2048]{1,0:T(8,128)(2,1)S(1)} %get-tuple-element.355), channel_id=1, source_target_pairs={{248,0},{0,8},{8,16},{16,24},{24,32},{32,40},{40,48},{48,56},{56,6... | collective-permute-start | bytes 589832 | tf_op jit(solution)/shard_map/while/body/eval_jaxpr/ppermute | solution.py:24
  162.9 7.3 %collective-permute-start.1 = (s32[48]{0:T(128)S(1)}, s32[48]{0:T(128)S(1)}, u32[]{:S(2)}, u32[]{:S(2)}) collective-permute-start(s32[48]{0:T(128)S(1)} %get-tuple-element.356), channel_id=1, source_target_pairs={{248,0},{0,8},{8,16},{16,24},{24,32},{32,40},{40,48},{48,56},{56,6... | collective-permute-start | bytes 584 | tf_op jit(solution)/shard_map/while/body/eval_jaxpr/ppermute | solution.py:24
  173.3 7.3 %collective-permute-start = (bf16[48,2048]{1,0:T(8,128)(2,1)S(1)}, bf16[48,2048]{1,0:T(8,128)(2,1)S(1)}, u32[]{:S(2)}, u32[]{:S(2)}) collective-permute-start(bf16[48,2048]{1,0:T(8,128)(2,1)S(1)} %get-tuple-element.355), channel_id=1, source_target_pairs={{248,0},{0,8},{8,16},{16,24},{24,32},{32,40},{40,48},{48,56},{56,6... | collective-permute-start | bytes 589832 | tf_op jit(solution)/shard_map/while/body/eval_jaxpr/ppermute | solution.py:24
  173.4 7.3 %collective-permute-start.1 = (s32[48]{0:T(128)S(1)}, s32[48]{0:T(128)S(1)}, u32[]{:S(2)}, u32[]{:S(2)}) collective-permute-start(s32[48]{0:T(128)S(1)} %get-tuple-element.356), channel_id=1, source_target_pairs={{248,0},{0,8},{8,16},{16,24},{24,32},{32,40},{40,48},{48,56},{56,6... | collective-permute-start | bytes 584 | tf_op jit(solution)/shard_map/while/body/eval_jaxpr/ppermute | solution.py:24
  183.8 7.3 %collective-permute-start = (bf16[48,2048]{1,0:T(8,128)(2,1)S(1)}, bf16[48,2048]{1,0:T(8,128)(2,1)S(1)}, u32[]{:S(2)}, u32[]{:S(2)}) collective-permute-start(bf16[48,2048]{1,0:T(8,128)(2,1)S(1)} %get-tuple-element.355), channel_id=1, source_target_pairs={{248,0},{0,8},{8,16},{16,24},{24,32},{32,40},{40,48},{48,56},{56,6... | collective-permute-start | bytes 589832 | tf_op jit(solution)/shard_map/while/body/eval_jaxpr/ppermute | solution.py:24
  183.9 7.3 %collective-permute-start.1 = (s32[48]{0:T(128)S(1)}, s32[48]{0:T(128)S(1)}, u32[]{:S(2)}, u32[]{:S(2)}) collective-permute-start(s32[48]{0:T(128)S(1)} %get-tuple-element.356), channel_id=1, source_target_pairs={{248,0},{0,8},{8,16},{16,24},{24,32},{32,40},{40,48},{48,56},{56,6... | collective-permute-start | bytes 584 | tf_op jit(solution)/shard_map/while/body/eval_jaxpr/ppermute | solution.py:24
  194.3 7.3 %collective-permute-start = (bf16[48,2048]{1,0:T(8,128)(2,1)S(1)}, bf16[48,2048]{1,0:T(8,128)(2,1)S(1)}, u32[]{:S(2)}, u32[]{:S(2)}) collective-permute-start(bf16[48,2048]{1,0:T(8,128)(2,1)S(1)} %get-tuple-element.355), channel_id=1, source_target_pairs={{248,0},{0,8},{8,16},{16,24},{24,32},{32,40},{40,48},{48,56},{56,6... | collective-permute-start | bytes 589832 | tf_op jit(solution)/shard_map/while/body/eval_jaxpr/ppermute | solution.py:24
  194.3 7.3 %collective-permute-start.1 = (s32[48]{0:T(128)S(1)}, s32[48]{0:T(128)S(1)}, u32[]{:S(2)}, u32[]{:S(2)}) collective-permute-start(s32[48]{0:T(128)S(1)} %get-tuple-element.356), channel_id=1, source_target_pairs={{248,0},{0,8},{8,16},{16,24},{24,32},{32,40},{40,48},{48,56},{56,6... | collective-permute-start | bytes 584 | tf_op jit(solution)/shard_map/while/body/eval_jaxpr/ppermute | solution.py:24
  204.7 7.3 %collective-permute-start = (bf16[48,2048]{1,0:T(8,128)(2,1)S(1)}, bf16[48,2048]{1,0:T(8,128)(2,1)S(1)}, u32[]{:S(2)}, u32[]{:S(2)}) collective-permute-start(bf16[48,2048]{1,0:T(8,128)(2,1)S(1)} %get-tuple-element.355), channel_id=1, source_target_pairs={{248,0},{0,8},{8,16},{16,24},{24,32},{32,40},{40,48},{48,56},{56,6... | collective-permute-start | bytes 589832 | tf_op jit(solution)/shard_map/while/body/eval_jaxpr/ppermute | solution.py:24
  204.8 7.3 %collective-permute-start.1 = (s32[48]{0:T(128)S(1)}, s32[48]{0:T(128)S(1)}, u32[]{:S(2)}, u32[]{:S(2)}) collective-permute-start(s32[48]{0:T(128)S(1)} %get-tuple-element.356), channel_id=1, source_target_pairs={{248,0},{0,8},{8,16},{16,24},{24,32},{32,40},{40,48},{48,56},{56,6... | collective-permute-start | bytes 584 | tf_op jit(solution)/shard_map/while/body/eval_jaxpr/ppermute | solution.py:24
  215.2 7.3 %collective-permute-start = (bf16[48,2048]{1,0:T(8,128)(2,1)S(1)}, bf16[48,2048]{1,0:T(8,128)(2,1)S(1)}, u32[]{:S(2)}, u32[]{:S(2)}) collective-permute-start(bf16[48,2048]{1,0:T(8,128)(2,1)S(1)} %get-tuple-element.355), channel_id=1, source_target_pairs={{248,0},{0,8},{8,16},{16,24},{24,32},{32,40},{40,48},{48,56},{56,6... | collective-permute-start | bytes 589832 | tf_op jit(solution)/shard_map/while/body/eval_jaxpr/ppermute | solution.py:24
  215.3 7.3 %collective-permute-start.1 = (s32[48]{0:T(128)S(1)}, s32[48]{0:T(128)S(1)}, u32[]{:S(2)}, u32[]{:S(2)}) collective-permute-start(s32[48]{0:T(128)S(1)} %get-tuple-element.356), channel_id=1, source_target_pairs={{248,0},{0,8},{8,16},{16,24},{24,32},{32,40},{40,48},{48,56},{56,6... | collective-permute-start | bytes 584 | tf_op jit(solution)/shard_map/while/body/eval_jaxpr/ppermute | solution.py:24
  225.7 7.3 %collective-permute-start = (bf16[48,2048]{1,0:T(8,128)(2,1)S(1)}, bf16[48,2048]{1,0:T(8,128)(2,1)S(1)}, u32[]{:S(2)}, u32[]{:S(2)}) collective-permute-start(bf16[48,2048]{1,0:T(8,128)(2,1)S(1)} %get-tuple-element.355), channel_id=1, source_target_pairs={{248,0},{0,8},{8,16},{16,24},{24,32},{32,40},{40,48},{48,56},{56,6... | collective-permute-start | bytes 589832 | tf_op jit(solution)/shard_map/while/body/eval_jaxpr/ppermute | solution.py:24
  225.8 7.3 %collective-permute-start.1 = (s32[48]{0:T(128)S(1)}, s32[48]{0:T(128)S(1)}, u32[]{:S(2)}, u32[]{:S(2)}) collective-permute-start(s32[48]{0:T(128)S(1)} %get-tuple-element.356), channel_id=1, source_target_pairs={{248,0},{0,8},{8,16},{16,24},{24,32},{32,40},{40,48},{48,56},{56,6... | collective-permute-start | bytes 584 | tf_op jit(solution)/shard_map/while/body/eval_jaxpr/ppermute | solution.py:24
  236.2 7.3 %collective-permute-start = (bf16[48,2048]{1,0:T(8,128)(2,1)S(1)}, bf16[48,2048]{1,0:T(8,128)(2,1)S(1)}, u32[]{:S(2)}, u32[]{:S(2)}) collective-permute-start(bf16[48,2048]{1,0:T(8,128)(2,1)S(1)} %get-tuple-element.355), channel_id=1, source_target_pairs={{248,0},{0,8},{8,16},{16,24},{24,32},{32,40},{40,48},{48,56},{56,6... | collective-permute-start | bytes 589832 | tf_op jit(solution)/shard_map/while/body/eval_jaxpr/ppermute | solution.py:24
  236.2 7.3 %collective-permute-start.1 = (s32[48]{0:T(128)S(1)}, s32[48]{0:T(128)S(1)}, u32[]{:S(2)}, u32[]{:S(2)}) collective-permute-start(s32[48]{0:T(128)S(1)} %get-tuple-element.356), channel_id=1, source_target_pairs={{248,0},{0,8},{8,16},{16,24},{24,32},{32,40},{40,48},{48,56},{56,6... | collective-permute-start | bytes 584 | tf_op jit(solution)/shard_map/while/body/eval_jaxpr/ppermute | solution.py:24
  246.6 7.3 %collective-permute-start = (bf16[48,2048]{1,0:T(8,128)(2,1)S(1)}, bf16[48,2048]{1,0:T(8,128)(2,1)S(1)}, u32[]{:S(2)}, u32[]{:S(2)}) collective-permute-start(bf16[48,2048]{1,0:T(8,128)(2,1)S(1)} %get-tuple-element.355), channel_id=1, source_target_pairs={{248,0},{0,8},{8,16},{16,24},{24,32},{32,40},{40,48},{48,56},{56,6... | collective-permute-start | bytes 589832 | tf_op jit(solution)/shard_map/while/body/eval_jaxpr/ppermute | solution.py:24
  246.7 7.3 %collective-permute-start.1 = (s32[48]{0:T(128)S(1)}, s32[48]{0:T(128)S(1)}, u32[]{:S(2)}, u32[]{:S(2)}) collective-permute-start(s32[48]{0:T(128)S(1)} %get-tuple-element.356), channel_id=1, source_target_pairs={{248,0},{0,8},{8,16},{16,24},{24,32},{32,40},{40,48},{48,56},{56,6... | collective-permute-start | bytes 584 | tf_op jit(solution)/shard_map/while/body/eval_jaxpr/ppermute | solution.py:24
  257.1 7.3 %collective-permute-start = (bf16[48,2048]{1,0:T(8,128)(2,1)S(1)}, bf16[48,2048]{1,0:T(8,128)(2,1)S(1)}, u32[]{:S(2)}, u32[]{:S(2)}) collective-permute-start(bf16[48,2048]{1,0:T(8,128)(2,1)S(1)} %get-tuple-element.355), channel_id=1, source_target_pairs={{248,0},{0,8},{8,16},{16,24},{24,32},{32,40},{40,48},{48,56},{56,6... | collective-permute-start | bytes 589832 | tf_op jit(solution)/shard_map/while/body/eval_jaxpr/ppermute | solution.py:24
  257.2 7.3 %collective-permute-start.1 = (s32[48]{0:T(128)S(1)}, s32[48]{0:T(128)S(1)}, u32[]{:S(2)}, u32[]{:S(2)}) collective-permute-start(s32[48]{0:T(128)S(1)} %get-tuple-element.356), channel_id=1, source_target_pairs={{248,0},{0,8},{8,16},{16,24},{24,32},{32,40},{40,48},{48,56},{56,6... | collective-permute-start | bytes 584 | tf_op jit(solution)/shard_map/while/body/eval_jaxpr/ppermute | solution.py:24
  267.6 7.3 %collective-permute-start = (bf16[48,2048]{1,0:T(8,128)(2,1)S(1)}, bf16[48,2048]{1,0:T(8,128)(2,1)S(1)}, u32[]{:S(2)}, u32[]{:S(2)}) collective-permute-start(bf16[48,2048]{1,0:T(8,128)(2,1)S(1)} %get-tuple-element.355), channel_id=1, source_target_pairs={{248,0},{0,8},{8,16},{16,24},{24,32},{32,40},{40,48},{48,56},{56,6... | collective-permute-start | bytes 589832 | tf_op jit(solution)/shard_map/while/body/eval_jaxpr/ppermute | solution.py:24
  267.7 7.3 %collective-permute-start.1 = (s32[48]{0:T(128)S(1)}, s32[48]{0:T(128)S(1)}, u32[]{:S(2)}, u32[]{:S(2)}) collective-permute-start(s32[48]{0:T(128)S(1)} %get-tuple-element.356), channel_id=1, source_target_pairs={{248,0},{0,8},{8,16},{16,24},{24,32},{32,40},{40,48},{48,56},{56,6... | collective-permute-start | bytes 584 | tf_op jit(solution)/shard_map/while/body/eval_jaxpr/ppermute | solution.py:24
  278.1 7.3 %collective-permute-start = (bf16[48,2048]{1,0:T(8,128)(2,1)S(1)}, bf16[48,2048]{1,0:T(8,128)(2,1)S(1)}, u32[]{:S(2)}, u32[]{:S(2)}) collective-permute-start(bf16[48,2048]{1,0:T(8,128)(2,1)S(1)} %get-tuple-element.355), channel_id=1, source_target_pairs={{248,0},{0,8},{8,16},{16,24},{24,32},{32,40},{40,48},{48,56},{56,6... | collective-permute-start | bytes 589832 | tf_op jit(solution)/shard_map/while/body/eval_jaxpr/ppermute | solution.py:24
  278.2 7.3 %collective-permute-start.1 = (s32[48]{0:T(128)S(1)}, s32[48]{0:T(128)S(1)}, u32[]{:S(2)}, u32[]{:S(2)}) collective-permute-start(s32[48]{0:T(128)S(1)} %get-tuple-element.356), channel_id=1, source_target_pairs={{248,0},{0,8},{8,16},{16,24},{24,32},{32,40},{40,48},{48,56},{56,6... | collective-permute-start | bytes 584 | tf_op jit(solution)/shard_map/while/body/eval_jaxpr/ppermute | solution.py:24
  288.5 7.3 %collective-permute-start = (bf16[48,2048]{1,0:T(8,128)(2,1)S(1)}, bf16[48,2048]{1,0:T(8,128)(2,1)S(1)}, u32[]{:S(2)}, u32[]{:S(2)}) collective-permute-start(bf16[48,2048]{1,0:T(8,128)(2,1)S(1)} %get-tuple-element.355), channel_id=1, source_target_pairs={{248,0},{0,8},{8,16},{16,24},{24,32},{32,40},{40,48},{48,56},{56,6... | collective-permute-start | bytes 589832 | tf_op jit(solution)/shard_map/while/body/eval_jaxpr/ppermute | solution.py:24
  288.6 7.3 %collective-permute-start.1 = (s32[48]{0:T(128)S(1)}, s32[48]{0:T(128)S(1)}, u32[]{:S(2)}, u32[]{:S(2)}) collective-permute-start(s32[48]{0:T(128)S(1)} %get-tuple-element.356), channel_id=1, source_target_pairs={{248,0},{0,8},{8,16},{16,24},{24,32},{32,40},{40,48},{48,56},{56,6... | collective-permute-start | bytes 584 | tf_op jit(solution)/shard_map/while/body/eval_jaxpr/ppermute | solution.py:24
  299.0 7.3 %collective-permute-start = (bf16[48,2048]{1,0:T(8,128)(2,1)S(1)}, bf16[48,2048]{1,0:T(8,128)(2,1)S(1)}, u32[]{:S(2)}, u32[]{:S(2)}) collective-permute-start(bf16[48,2048]{1,0:T(8,128)(2,1)S(1)} %get-tuple-element.355), channel_id=1, source_target_pairs={{248,0},{0,8},{8,16},{16,24},{24,32},{32,40},{40,48},{48,56},{56,6... | collective-permute-start | bytes 589832 | tf_op jit(solution)/shard_map/while/body/eval_jaxpr/ppermute | solution.py:24
  299.1 7.3 %collective-permute-start.1 = (s32[48]{0:T(128)S(1)}, s32[48]{0:T(128)S(1)}, u32[]{:S(2)}, u32[]{:S(2)}) collective-permute-start(s32[48]{0:T(128)S(1)} %get-tuple-element.356), channel_id=1, source_target_pairs={{248,0},{0,8},{8,16},{16,24},{24,32},{32,40},{40,48},{48,56},{56,6... | collective-permute-start | bytes 584 | tf_op jit(solution)/shard_map/while/body/eval_jaxpr/ppermute | solution.py:24
  309.5 7.3 %collective-permute-start = (bf16[48,2048]{1,0:T(8,128)(2,1)S(1)}, bf16[48,2048]{1,0:T(8,128)(2,1)S(1)}, u32[]{:S(2)}, u32[]{:S(2)}) collective-permute-start(bf16[48,2048]{1,0:T(8,128)(2,1)S(1)} %get-tuple-element.355), channel_id=1, source_target_pairs={{248,0},{0,8},{8,16},{16,24},{24,32},{32,40},{40,48},{48,56},{56,6... | collective-permute-start | bytes 589832 | tf_op jit(solution)/shard_map/while/body/eval_jaxpr/ppermute | solution.py:24
  309.6 7.3 %collective-permute-start.1 = (s32[48]{0:T(128)S(1)}, s32[48]{0:T(128)S(1)}, u32[]{:S(2)}, u32[]{:S(2)}) collective-permute-start(s32[48]{0:T(128)S(1)} %get-tuple-element.356), channel_id=1, source_target_pairs={{248,0},{0,8},{8,16},{16,24},{24,32},{32,40},{40,48},{48,56},{56,6... | collective-permute-start | bytes 584 | tf_op jit(solution)/shard_map/while/body/eval_jaxpr/ppermute | solution.py:24
  320.0 7.3 %collective-permute-start = (bf16[48,2048]{1,0:T(8,128)(2,1)S(1)}, bf16[48,2048]{1,0:T(8,128)(2,1)S(1)}, u32[]{:S(2)}, u32[]{:S(2)}) collective-permute-start(bf16[48,2048]{1,0:T(8,128)(2,1)S(1)} %get-tuple-element.355), channel_id=1, source_target_pairs={{248,0},{0,8},{8,16},{16,24},{24,32},{32,40},{40,48},{48,56},{56,6... | collective-permute-start | bytes 589832 | tf_op jit(solution)/shard_map/while/body/eval_jaxpr/ppermute | solution.py:24
  320.1 7.3 %collective-permute-start.1 = (s32[48]{0:T(128)S(1)}, s32[48]{0:T(128)S(1)}, u32[]{:S(2)}, u32[]{:S(2)}) collective-permute-start(s32[48]{0:T(128)S(1)} %get-tuple-element.356), channel_id=1, source_target_pairs={{248,0},{0,8},{8,16},{16,24},{24,32},{32,40},{40,48},{48,56},{56,6... | collective-permute-start | bytes 584 | tf_op jit(solution)/shard_map/while/body/eval_jaxpr/ppermute | solution.py:24
  330.4 7.3 %collective-permute-start = (bf16[48,2048]{1,0:T(8,128)(2,1)S(1)}, bf16[48,2048]{1,0:T(8,128)(2,1)S(1)}, u32[]{:S(2)}, u32[]{:S(2)}) collective-permute-start(bf16[48,2048]{1,0:T(8,128)(2,1)S(1)} %get-tuple-element.355), channel_id=1, source_target_pairs={{248,0},{0,8},{8,16},{16,24},{24,32},{32,40},{40,48},{48,56},{56,6... | collective-permute-start | bytes 589832 | tf_op jit(solution)/shard_map/while/body/eval_jaxpr/ppermute | solution.py:24
  330.5 7.3 %collective-permute-start.1 = (s32[48]{0:T(128)S(1)}, s32[48]{0:T(128)S(1)}, u32[]{:S(2)}, u32[]{:S(2)}) collective-permute-start(s32[48]{0:T(128)S(1)} %get-tuple-element.356), channel_id=1, source_target_pairs={{248,0},{0,8},{8,16},{16,24},{24,32},{32,40},{40,48},{48,56},{56,6... | collective-permute-start | bytes 584 | tf_op jit(solution)/shard_map/while/body/eval_jaxpr/ppermute | solution.py:24
  340.9 7.3 %collective-permute-start = (bf16[48,2048]{1,0:T(8,128)(2,1)S(1)}, bf16[48,2048]{1,0:T(8,128)(2,1)S(1)}, u32[]{:S(2)}, u32[]{:S(2)}) collective-permute-start(bf16[48,2048]{1,0:T(8,128)(2,1)S(1)} %get-tuple-element.355), channel_id=1, source_target_pairs={{248,0},{0,8},{8,16},{16,24},{24,32},{32,40},{40,48},{48,56},{56,6... | collective-permute-start | bytes 589832 | tf_op jit(solution)/shard_map/while/body/eval_jaxpr/ppermute | solution.py:24
  341.0 7.3 %collective-permute-start.1 = (s32[48]{0:T(128)S(1)}, s32[48]{0:T(128)S(1)}, u32[]{:S(2)}, u32[]{:S(2)}) collective-permute-start(s32[48]{0:T(128)S(1)} %get-tuple-element.356), channel_id=1, source_target_pairs={{248,0},{0,8},{8,16},{16,24},{24,32},{32,40},{40,48},{48,56},{56,6... | collective-permute-start | bytes 584 | tf_op jit(solution)/shard_map/while/body/eval_jaxpr/ppermute | solution.py:24
  351.4 7.3 %collective-permute-start = (bf16[48,2048]{1,0:T(8,128)(2,1)S(1)}, bf16[48,2048]{1,0:T(8,128)(2,1)S(1)}, u32[]{:S(2)}, u32[]{:S(2)}) collective-permute-start(bf16[48,2048]{1,0:T(8,128)(2,1)S(1)} %get-tuple-element.355), channel_id=1, source_target_pairs={{248,0},{0,8},{8,16},{16,24},{24,32},{32,40},{40,48},{48,56},{56,6... | collective-permute-start | bytes 589832 | tf_op jit(solution)/shard_map/while/body/eval_jaxpr/ppermute | solution.py:24
  351.5 7.3 %collective-permute-start.1 = (s32[48]{0:T(128)S(1)}, s32[48]{0:T(128)S(1)}, u32[]{:S(2)}, u32[]{:S(2)}) collective-permute-start(s32[48]{0:T(128)S(1)} %get-tuple-element.356), channel_id=1, source_target_pairs={{248,0},{0,8},{8,16},{16,24},{24,32},{32,40},{40,48},{48,56},{56,6... | collective-permute-start | bytes 584 | tf_op jit(solution)/shard_map/while/body/eval_jaxpr/ppermute | solution.py:24
  361.9 7.3 %collective-permute-start = (bf16[48,2048]{1,0:T(8,128)(2,1)S(1)}, bf16[48,2048]{1,0:T(8,128)(2,1)S(1)}, u32[]{:S(2)}, u32[]{:S(2)}) collective-permute-start(bf16[48,2048]{1,0:T(8,128)(2,1)S(1)} %get-tuple-element.355), channel_id=1, source_target_pairs={{248,0},{0,8},{8,16},{16,24},{24,32},{32,40},{40,48},{48,56},{56,6... | collective-permute-start | bytes 589832 | tf_op jit(solution)/shard_map/while/body/eval_jaxpr/ppermute | solution.py:24
  362.0 7.3 %collective-permute-start.1 = (s32[48]{0:T(128)S(1)}, s32[48]{0:T(128)S(1)}, u32[]{:S(2)}, u32[]{:S(2)}) collective-permute-start(s32[48]{0:T(128)S(1)} %get-tuple-element.356), channel_id=1, source_target_pairs={{248,0},{0,8},{8,16},{16,24},{24,32},{32,40},{40,48},{48,56},{56,6... | collective-permute-start | bytes 584 | tf_op jit(solution)/shard_map/while/body/eval_jaxpr/ppermute | solution.py:24
  372.3 7.3 %collective-permute-start = (bf16[48,2048]{1,0:T(8,128)(2,1)S(1)}, bf16[48,2048]{1,0:T(8,128)(2,1)S(1)}, u32[]{:S(2)}, u32[]{:S(2)}) collective-permute-start(bf16[48,2048]{1,0:T(8,128)(2,1)S(1)} %get-tuple-element.355), channel_id=1, source_target_pairs={{248,0},{0,8},{8,16},{16,24},{24,32},{32,40},{40,48},{48,56},{56,6... | collective-permute-start | bytes 589832 | tf_op jit(solution)/shard_map/while/body/eval_jaxpr/ppermute | solution.py:24
  372.4 7.3 %collective-permute-start.1 = (s32[48]{0:T(128)S(1)}, s32[48]{0:T(128)S(1)}, u32[]{:S(2)}, u32[]{:S(2)}) collective-permute-start(s32[48]{0:T(128)S(1)} %get-tuple-element.356), channel_id=1, source_target_pairs={{248,0},{0,8},{8,16},{16,24},{24,32},{32,40},{40,48},{48,56},{56,6... | collective-permute-start | bytes 584 | tf_op jit(solution)/shard_map/while/body/eval_jaxpr/ppermute | solution.py:24
  382.8 7.3 %collective-permute-start = (bf16[48,2048]{1,0:T(8,128)(2,1)S(1)}, bf16[48,2048]{1,0:T(8,128)(2,1)S(1)}, u32[]{:S(2)}, u32[]{:S(2)}) collective-permute-start(bf16[48,2048]{1,0:T(8,128)(2,1)S(1)} %get-tuple-element.355), channel_id=1, source_target_pairs={{248,0},{0,8},{8,16},{16,24},{24,32},{32,40},{40,48},{48,56},{56,6... | collective-permute-start | bytes 589832 | tf_op jit(solution)/shard_map/while/body/eval_jaxpr/ppermute | solution.py:24
  382.9 7.3 %collective-permute-start.1 = (s32[48]{0:T(128)S(1)}, s32[48]{0:T(128)S(1)}, u32[]{:S(2)}, u32[]{:S(2)}) collective-permute-start(s32[48]{0:T(128)S(1)} %get-tuple-element.356), channel_id=1, source_target_pairs={{248,0},{0,8},{8,16},{16,24},{24,32},{32,40},{40,48},{48,56},{56,6... | collective-permute-start | bytes 584 | tf_op jit(solution)/shard_map/while/body/eval_jaxpr/ppermute | solution.py:24
Sparse Core Ops, SparseCore 0:
  10.0 54.4 all-gather.1
where the time goes:
time: 438 us
  waiting for transfers between devices  248 us (57%)
  other arithmetic  73.4 us (17%)
  blocking collectives  47.4 us (11%)
  local copies, waits for them, and re-layouts  24.4 us (6%)
  between operations  19.4 us (4%)
  matrix products  16.1 us (4%)
  starting transfers between devices  6.66 us (2%)
    ppermute x62, waiting for transfers between devices, from_behind(): return lax.ppermute(block, axis, route)  216 us
    sort x33, other arithmetic, best_values(): ordered = -jnp.sort(-values, axis=1)  63.2 us
    all_gather x1, blocking collectives, local(): pooled = lax.all_gather(best, 'grp', axis=1, tiled=True)  34.2 us
    all_gather x1, waiting for transfers between devices, local(): lax.all_gather(queries, 'grp', axis=0, tiled=True)  32.7 us
    dot_general x32, matrix products, fold_in(): lax.dot_general(group_q, stacked, (((1,), (1,)), ((), ())), preferred_ele...  16.1 us
    unnamed x1, blocking collectives  13.2 us
    dynamic_slice x32, local copies, waits for them, and re-layouts, shifted_stack(): lax.dynamic_slice_in_dim(padded, MAXSHIFT - shifts[index], BINS, 1)  12.6 us
  transfers between devices with their start and end apart: 63, of which 32 were waited for; matrix products, arithmetic and copies ran while one was open for 2% of the time, Pallas kernels for 0%

commit v1 on v0

v1 whole, which is shorter than its diff:
```python
import functools
import math

import jax
import jax.numpy as jnp
from jax import lax
from jax.experimental import pallas as pl
from jax.experimental.pallas import tpu as pltpu
from jax.sharding import PartitionSpec as P

BINS = 2048
NOFF = 4
TOPK = 16
MAXSHIFT = 24
QBLK = 16
LBLK = 8
SPAN = 4
EPS = 1e-06
MASKED = -8.0

QD = 32
LD = 48
CH = 16
NQ = 16 * QD
NL = 16 * LD
PAD = BINS + 2 * MAXSHIFT
MESH = pl.DeviceIdType.MESH

SLOTS = [
    (0, 0), (1, 0), (3, 0), (2, 0),
    (0, 1), (0, 3), (1, 1), (1, 3),
    (3, 1), (3, 3), (2, 1), (2, 3),
    (0, 2), (1, 2), (3, 2), (2, 2),
]


def qslot(a, b):
    return SLOTS.index((a % 4, b % 4))


def lplace(dz, c):
    dz %= 8
    if dz == 0:
        return c
    if dz == 4:
        return 14 + c
    d = min(dz, 8 - dz)
    return 2 + 4 * (d - 1) + 2 * c + (1 if dz > 4 else 0)


def batcher(n):
    pairs = []
    p = 1
    while p < n:
        k = p
        while k >= 1:
            for j in range(k % p, n - k, 2 * k):
                for i in range(min(k, n - j - k)):
                    if (i + j) // (2 * p) == (i + j + k) // (2 * p):
                        pairs.append((i + j, i + j + k))
            k //= 2
        p *= 2
    return pairs


SORT16 = batcher(16)


def sort16(v):
    v = list(v)
    for i, j in SORT16:
        v[i], v[j] = jnp.maximum(v[i], v[j]), jnp.minimum(v[i], v[j])
    return v


def merge16(a, b):
    v = [jnp.maximum(a[i], b[15 - i]) for i in range(16)]
    for d in (8, 4, 2, 1):
        for i in range(16):
            if not i & d:
                v[i], v[i + d] = jnp.maximum(v[i], v[i + d]), jnp.minimum(v[i], v[i + d])
    return v


def kernel(
    q_in, w_in, l_in, b_in, s_in, out,
    qbuf, lbuf, qt32, qtk, sc, lsc, lband, qrow, best, lmeta, qmeta, fin, got,
    loc_sem, qs_sem, qr_sem, ls_sem, lr_sem, ss_sem, sr_sem, m_sem, f_sem,
):
    blk = lax.axis_index("blk")
    grp = lax.axis_index("grp")
    core = lax.rem(blk, 2)
    z = lax.rem(lax.div(blk, 2), 8)
    x = lax.div(grp, 2)
    y = lax.rem(grp, 2) * 2 + lax.div(blk, 16)

    def place(px, py, pz, pc):
        return {
            "blk": (lax.rem(py, 2) * 8 + pz) * 2 + pc,
            "grp": px * 2 + lax.div(py, 2),
        }

    def plane(a, b):
        dx = a * (1 - core) + b * core
        dy = b * (1 - core) + a * core
        return place(lax.rem(x + dx, 4), lax.rem(y + dy, 4), z, core)

    def column(dz, dc):
        return place(x, y, lax.rem(z + dz, 8), core + dc * (1 - 2 * core))

    barrier = pltpu.get_barrier_semaphore()
    peers_p = [(a % 4, b % 4) for a, b in SLOTS[1:]]
    peers_c = [(dz, dc) for dc in range(2) for dz in range(8) if (dz, dc) != (0, 0)]
    for a, b in peers_p:
        pl.semaphore_signal(barrier, inc=1, device_id=plane(a, b), device_id_type=MESH)
    for dz, dc in peers_c:
        pl.semaphore_signal(barrier, inc=1, device_id=column(dz, dc), device_id_type=MESH)
    loc_q = pltpu.make_async_copy(q_in, qbuf.at[pl.ds(0, QD)], loc_sem.at[0])
    loc_l = pltpu.make_async_copy(l_in, lbuf.at[pl.ds(0, LD)], loc_sem.at[1])
    loc_q.start()
    loc_l.start()
    pl.semaphore_wait(barrier, 30)

    sends = []

    def lrows(dz, chunk):
        return lbuf.at[pl.ds(LD * lplace(dz, 0) + CH * chunk, CH)]

    def lsem(dz, chunk):
        return ((dz - 1) * 3) + chunk

    def l_send(src, dst_dz, chunk, step):
        n = lsem(dst_dz % 8, chunk)
        c = pltpu.make_async_remote_copy(
            src_ref=src, dst_ref=lrows(dst_dz, chunk), send_sem=ls_sem.at[n],
            recv_sem=lr_sem.at[n], device_id=column(step, 0), device_id_type=MESH,
        )
        c.start()
        sends.append(c)

    def l_wait(dz, chunk):
        n = lsem(dz % 8, chunk)
        ref = lrows(dz, chunk)
        pltpu.make_async_copy(ref, ref, lr_sem.at[n]).wait()

    def l_forward(d, chunk):
        l_wait(8 - d, chunk)
        l_wait(d, chunk)
        if d < 3:
            l_send(lrows(8 - d, chunk), 7 - d, chunk, 1)
            l_send(lrows(d, chunk), d + 1, chunk, 7)
        elif chunk == 0:
            l_send(lrows(5, 0), 4, 0, 1)
        elif chunk == 2:
            l_send(lrows(3, 2), 4, 2, 7)
        else:
            row = LD * (lplace(5, 0) * (1 - core) + lplace(3, 0) * core) + CH
            src = lbuf.at[pl.ds(pl.multiple_of(row, CH), CH)]
            l_send(src, 4, 1, 1 + 6 * core)

    def sib(src, dz):
        c = pltpu.make_async_remote_copy(
            src_ref=src, dst_ref=lbuf.at[pl.ds(LD * lplace(dz, 1), LD)],
            send_sem=ss_sem.at[dz], recv_sem=sr_sem.at[dz],
            device_id=column(0, 1), device_id_type=MESH,
        )
        c.start()
        sends.append(c)

    def sib_forward(dz):
        sib(lbuf.at[pl.ds(LD * lplace(dz, 0), LD)], dz)

    def sib_wait(dz):
        ref = lbuf.at[pl.ds(LD * lplace(dz, 1), LD)]
        pltpu.make_async_copy(ref, ref, sr_sem.at[dz]).wait()

    def qrows(a, b, half=None):
        s = QD * qslot(a, b)
        if half is None:
            return qbuf.at[pl.ds(s, QD)]
        return qbuf.at[pl.ds(s + 16 * half, 16)]

    def qsem(a, b, half):
        return qslot(a, b) * 2 + (half or 0)

    def q_send(src, a, b, half, to):
        n = qsem(a, b, half)
        c = pltpu.make_async_remote_copy(
            src_ref=src, dst_ref=qrows(a, b, half), send_sem=qs_sem.at[n],
            recv_sem=qr_sem.at[n], device_id=plane(*to), device_id_type=MESH,
        )
        c.start()
        sends.append(c)

    def q_wait(a, b, half=None):
        ref = qrows(a, b, half)
        pltpu.make_async_copy(ref, ref, qr_sem.at[qsem(a, b, half)]).wait()

    for chunk in range(3):
        src = l_in.at[pl.ds(CH * chunk, CH)]
        l_send(src, 7, chunk, 1)
        l_send(src, 1, chunk, 7)
        if chunk == 0:
            q_send(q_in, 3, 0, None, (1, 0))
            q_send(q_in, 1, 0, None, (3, 0))
            q_send(q_in, 0, 3, None, (0, 1))
            q_send(q_in, 0, 1, None, (0, 3))
    sib(l_in, 0)

    lane = lax.broadcasted_iota(jnp.int32, (1, 128), 1)

    def squares(ref, rows):
        acc = jnp.zeros((rows, 128), jnp.float32)
        for t in range(BINS // 128):
            v = ref[0:rows, 128 * t:128 * (t + 1)].astype(jnp.float32)
            acc = acc + v * v
        return acc

    def scale(total):
        return lax.rsqrt(jnp.sum(total.T, axis=0, keepdims=True) * (1.0 / BINS) + EPS)

    loc_q.wait()
    acc = squares(qbuf, QD)
    qscale = scale(jnp.concatenate([acc] * 4, axis=0)) * (1.0 / math.sqrt(BINS))
    first = lax.rem(lane, QD) < QBLK
    qwin = jnp.where(first, w_in[0], w_in[1]).astype(jnp.float32)
    qmeta[0, 0:1, :] = qscale
    qmeta[0, 1:2, :] = qwin
    loc_l.wait()
    acc = squares(lbuf, LD)
    lscale = scale(jnp.concatenate([acc, jnp.zeros((128 - LD, 128), jnp.float32)], axis=0))
    row_band = jnp.zeros((1, 128), jnp.int32)
    for j in range(LD // LBLK):
        row_band = jnp.where(lane >= 64 + LBLK * j, b_in[j], row_band)
    lmeta[0] = jnp.where(lane < 64, lscale, row_band.astype(jnp.float32))

    for a, b in peers_p:
        pltpu.make_async_remote_copy(
            src_ref=qmeta.at[0], dst_ref=qmeta.at[qslot(-a, -b)], send_sem=m_sem.at[0],
            recv_sem=m_sem.at[1], device_id=plane(a, b), device_id_type=MESH,
        ).start()
    for dz, dc in peers_c:
        pltpu.make_async_remote_copy(
            src_ref=lmeta.at[0], dst_ref=lmeta.at[lplace(-dz, dc)], send_sem=m_sem.at[2],
            recv_sem=m_sem.at[3], device_id=column(dz, dc), device_id_type=MESH,
        ).start()

    qt32[:, 0:MAXSHIFT, :] = jnp.zeros((4, MAXSHIFT, 128), jnp.float32)
    qt32[:, BINS + MAXSHIFT:PAD, :] = jnp.zeros((4, MAXSHIFT, 128), jnp.float32)
    best[...] = jnp.full(best.shape, -jnp.inf, jnp.float32)

    eye_r = lax.broadcasted_iota(jnp.int32, (256, 256), 0)
    eye_c = lax.broadcasted_iota(jnp.int32, (256, 256), 1)
    eye = (eye_r == eye_c).astype(jnp.float32).astype(jnp.bfloat16)

    def prepare(h):
        @pl.loop(0, BINS // 256)
        def _(i):
            c0 = pl.multiple_of(i * 256, 256)
            t = lax.dot_general(
                eye, qbuf[256 * h:256 * h + 256, pl.ds(c0, 256)],
                (((1,), (1,)), ((), ())), preferred_element_type=jnp.float32,
            )
            r0 = pl.multiple_of(MAXSHIFT + c0, 8)
            qt32[2 * h, pl.ds(r0, 256), :] = t[:, 0:128]
            qt32[2 * h + 1, pl.ds(r0, 256), :] = t[:, 128:256]

        for k in range(NOFF):
            off = s_in[k] + MAXSHIFT

            @pl.loop(0, BINS // 128)
            def _(i):
                r0 = pl.multiple_of(i * 128, 128)
                for t in range(2):
                    v = qt32[2 * h + t, pl.ds(r0 + off, 128), :]
                    c0 = 256 * h + 128 * t
                    qtk[k, pl.ds(r0, 128), c0:c0 + 128] = v.astype(jnp.bfloat16)

    def multiply(row, rows, h):
        cols = slice(256 * h, 256 * h + 256)
        for k in range(NOFF):
            d = jnp.dot(
                lbuf[row:row + rows, :], qtk[k, :, cols], preferred_element_type=jnp.float32
            )
            if k:
                d = jnp.maximum(sc[row:row + rows, cols], d)
            sc[row:row + rows, cols] = d

    def select(g0, g1):
        @pl.loop(g0, g1)
        def _(g):
            for t in range(4):
                cols = slice(128 * t, 128 * t + 128)
                scale_q = jnp.broadcast_to(qrow[0:1, cols], (8, 128))
                low = jnp.broadcast_to(qrow[1:2, cols], (8, 128))
                high = low + float(SPAN)
                vals = []
                for i in range(16):
                    r = pl.multiple_of(g * 128 + 8 * i, 8)
                    band = lband[pl.ds(r, 8), :]
                    v = sc[pl.ds(r, 8), cols] * scale_q * lsc[pl.ds(r, 8), :]
                    keep = (band >= low) & (band < high)
                    vals.append(jnp.where(keep, v, MASKED))
                vals = sort16(vals)
                vals = merge16([best[t, i] for i in range(16)], vals)
                for i in range(16):
                    best[t, i] = vals[i]

    l_forward(1, 0)
    q_wait(1, 0)
    q_wait(3, 0)
    q_send(qrows(1, 0, 1), 2, 0, 1, (3, 0))
    q_send(qrows(3, 0, 0), 2, 0, 0, (1, 0))
    for a in (1, 3):
        q_send(qrows(a, 0), a, 3, None, (0, 1))
        q_send(qrows(a, 0), a, 1, None, (0, 3))
    l_forward(1, 1)

    def q_far(a):
        q_wait(a, 1)
        q_wait(a, 3)
        q_send(qrows(a, 1, 1), a, 2, 1, (0, 3))
        q_send(qrows(a, 3, 0), a, 2, 0, (0, 1))

    q_wait(2, 0, 0)
    q_wait(2, 0, 1)
    q_send(qrows(2, 0), 2, 3, None, (0, 1))
    q_send(qrows(2, 0), 2, 1, None, (0, 3))
    q_far(0)
    l_forward(1, 2)
    sib_forward(1)
    sib_forward(7)
    q_far(1)
    l_forward(2, 0)
    prepare(0)
    l_forward(2, 1)
    q_far(3)
    for dz in (0, 1, 7):
        sib_wait(dz)
    multiply(0, 288, 0)
    l_forward(2, 2)
    sib_forward(2)
    sib_forward(6)
    q_far(2)

    pltpu.make_async_copy(lmeta.at[pl.ds(1, 15)], lmeta.at[pl.ds(1, 15)], m_sem.at[3]).wait()
    pltpu.make_async_copy(qmeta.at[pl.ds(1, 15)], qmeta.at[pl.ds(1, 15)], m_sem.at[1]).wait()

    @pl.loop(0, 16)
    def _(i):
        m = jnp.broadcast_to(lmeta[i], (128, 128)).T
        r = pl.multiple_of(i * LD, 8)
        lsc[pl.ds(r, LD), :] = m[0:LD]
        lband[pl.ds(r, LD), :] = m[64:64 + LD]

    part = lax.div(lax.broadcasted_iota(jnp.int32, (2, 128), 1), QD)
    for t in range(4):
        m = qmeta[4 * t]
        for p in range(1, 4):
            m = jnp.where(part == p, qmeta[4 * t + p], m)
        qrow[0:2, 128 * t:128 * t + 128] = m

    l_forward(3, 0)
    sib_wait(2)
    sib_wait(6)
    multiply(288, 192, 0)
    for a in (0, 1, 3, 2):
        q_wait(a, 2, 0)
        q_wait(a, 2, 1)
    l_forward(3, 1)
    prepare(1)
    l_forward(3, 2)
    sib_forward(3)
    sib_forward(5)
    multiply(0, 288, 1)
    multiply(288, 192, 1)
    select(0, 3)
    for chunk in range(3):
        l_wait(4, chunk)
    sib_forward(4)
    sib_wait(3)
    sib_wait(5)
    for h in range(2):
        multiply(480, 192, h)
    select(3, 5)
    sib_wait(4)
    for h in range(2):
        multiply(672, 96, h)
    select(5, 6)

    for t in range(4):
        vals = [best[t, i] for i in range(16)]
        for sh in (4, 2, 1):
            vals = merge16(vals, [pltpu.roll(v, sh, 0) for v in vals])
        for i in range(16):
            fin[t, i:i + 1, :] = vals[i][0:1]
        for p in range(4):
            n = 4 * t + p
            if n == 0:
                continue
            a, b = SLOTS[n]
            pltpu.make_async_remote_copy(
                src_ref=fin.at[t], dst_ref=got.at[n], send_sem=f_sem.at[0],
                recv_sem=f_sem.at[1], device_id=plane(a, b), device_id_type=MESH,
            ).start()
    got[0] = fin[0]
    for c in sends:
        c.wait_send()
    pltpu.make_async_copy(qmeta.at[pl.ds(1, 15)], qmeta.at[pl.ds(1, 15)], m_sem.at[0]).wait()
    pltpu.make_async_copy(lmeta.at[pl.ds(1, 15)], lmeta.at[pl.ds(1, 15)], m_sem.at[2]).wait()
    pltpu.make_async_copy(got.at[pl.ds(1, 15)], got.at[pl.ds(1, 15)], f_sem.at[0]).wait()
    pltpu.make_async_copy(got.at[pl.ds(1, 15)], got.at[pl.ds(1, 15)], f_sem.at[1]).wait()

    part = lax.div(lax.broadcasted_iota(jnp.int32, (8, 128), 1), QD)
    vals = []
    for r in range(16):
        rows = []
        for t in range(4):
            v = got[4 * t, r:r + 1, :]
            for p in range(1, 4):
                v = jnp.where(part[0:1] == p, got[4 * t + p, r:r + 1, :], v)
            rows.append(v)
        vals.append(jnp.concatenate(rows + rows, axis=0))
    for sh in (2, 1):
        vals = merge16(vals, [pltpu.roll(v, sh, 0) for v in vals])
    for sh in (64, 32):
        vals = merge16(vals, [pltpu.roll(v, sh, 1) for v in vals])
    full = jnp.concatenate([v[0:1] for v in vals] + [jnp.zeros((112, 128), jnp.float32)], axis=0)
    out[...] = full.T[0:QD, 0:TOPK]


def local(queries, windows, library, bands, shifts):
    dma = pltpu.SemaphoreType.DMA
    f32, bf16 = jnp.float32, jnp.bfloat16
    hbm = pl.BlockSpec(memory_space=pl.ANY)
    smem = pl.BlockSpec(memory_space=pltpu.SMEM)
    return pl.pallas_call(
        kernel,
        out_shape=jax.ShapeDtypeStruct((QD, TOPK), f32),
        in_specs=[hbm, smem, hbm, smem, smem],
        out_specs=pl.BlockSpec(memory_space=pltpu.VMEM),
        scratch_shapes=[
            pltpu.VMEM((NQ, BINS), bf16),
            pltpu.VMEM((NL, BINS), bf16),
            pltpu.VMEM((4, PAD, 128), f32),
            pltpu.VMEM((NOFF, BINS, NQ), bf16),
            pltpu.VMEM((NL, NQ), f32),
            pltpu.VMEM((NL, 128), f32),
            pltpu.VMEM((NL, 128), f32),
            pltpu.VMEM((8, NQ), f32),
            pltpu.VMEM((4, 16, 8, 128), f32),
            pltpu.VMEM((16, 1, 128), f32),
            pltpu.VMEM((16, 2, 128), f32),
            pltpu.VMEM((4, 16, 128), f32),
            pltpu.VMEM((16, 16, 128), f32),
            dma((2,)), dma((32,)), dma((32,)), dma((21,)), dma((21,)),
            dma((8,)), dma((8,)), dma((4,)), dma((2,)),
        ],
        compiler_params=pltpu.CompilerParams(
            collective_id=0, has_side_effects=True, vmem_limit_bytes=48 * 2**20
        ),
        cost_estimate=pl.CostEstimate(
            flops=2 * NQ * NL * BINS * NOFF, bytes_accessed=2 * (QD + LD) * BINS, transcendentals=0
        ),
    )(queries, windows, library, bands, shifts)


def solution(mesh):
    return jax.shard_map(
        local,
        mesh=mesh,
        in_specs=(
            P(("blk", "grp"), None),
            P(("blk", "grp")),
            P(("blk", "grp"), None),
            P(("blk", "grp")),
            P(),
        ),
        out_specs=P(("blk", "grp"), None),
        check_vma=False,
    )
```

time: 438 us -> 48.6 us (0.11)
  the two profiles are of different devices: /device:TPU:8 before, /device:TPU:1 now
where the time goes in v1:
time: 48.6 us; the launch traced here: 48.5 us
  Pallas kernels  44 us (91%)
  local copies, waits for them, and re-layouts  4.46 us (9%)
    pallas_call x1, Pallas kernels, local(): pl.pallas_call(kernel, out_shape=jax.ShapeDtypeStruct((QD, TOPK), f32), i...  44 us
    unnamed x10, local copies, waits for them, and re-layouts  3.79 us

profile of v1, /device:TPU:1, one launch (start us, length us, event | category | flops | bytes accessed | tf_op | source)
XLA Modules:
  0.0 48.5 jit_solution(8826080461236562027)
XLA Ops:
  0.0 0.0 copy-start
  0.0 0.9 %copy-done = bf16[48,2048]{1,0:T(8,128)(2,1)S(1)} copy-done((bf16[48,2048]{1,0:T(8,128)(2,1)S(1)}, bf16[48,2048]{1,0:T(8,128)(2,1)}, u32[]{:S(2)}) %copy-start) | copy-done | bytes 196632
  0.9 0.0 copy-start.1
  0.9 0.9 %copy-done.1 = bf16[32,2048]{1,0:T(8,128)(2,1)S(1)} copy-done((bf16[32,2048]{1,0:T(8,128)(2,1)S(1)}, bf16[32,2048]{1,0:T(8,128)(2,1)}, u32[]{:S(2)}) %copy-start.1) | copy-done | bytes 131096
  1.8 0.0 copy-start.2
  1.8 0.7 %copy-done.2 = s32[2]{0:T(128)S(1)} copy-done((s32[2]{0:T(128)S(1)}, s32[2]{0:T(128)}, u32[]{:S(2)}) %copy-start.2) | copy-done | bytes 32
  2.5 0.0 copy-start.3
  2.5 0.7 %copy-done.3 = s32[6]{0:T(128)S(1)} copy-done((s32[6]{0:T(128)S(1)}, s32[6]{0:T(128)}, u32[]{:S(2)}) %copy-start.3) | copy-done | bytes 48
  3.1 0.0 copy-start.4
  3.1 0.7 %copy-done.4 = s32[4]{0:T(128)S(1)} copy-done((s32[4]{0:T(128)S(1)}, s32[4]{0:T(128)}, u32[]{:S(2)}) %copy-start.4) | copy-done | bytes 40
  3.8 44.0 %shard_map.55 = f32[32,16]{1,0:T(8,128)S(1)} custom-call(bf16[32,2048]{1,0:T(8,128)(2,1)S(1)} %copy-done.1, s32[2]{0:T(128)S(1)} %copy-done.2, bf16[48,2048]{1,0:T(8,128)(2,1)S(1)} %copy-done, s32[6]{0:T(128)S(1)} %copy-done.3, s32[4]{0:T(128)S(1)} %copy-done.4), custom_call_target="tpu_custom_call" | custom-call | flops 6442450944 | bytes 327680 | tf_op jit(solution)/shard_map/pallas_call | solution.py:437
  47.8 0.7 %copy.6 = f32[32,16]{0,1:T(8,128)} copy(f32[32,16]{1,0:T(8,128)S(1)} %shard_map.55) | data formatting | bytes 4096 | tf_op jit(solution)/shard_map/pallas_call | solution.py:437
Async XLA Ops:
  0.0 0.9 %copy-start = (bf16[48,2048]{1,0:T(8,128)(2,1)S(1)}, bf16[48,2048]{1,0:T(8,128)(2,1)}, u32[]{:S(2)}) copy-start(bf16[48,2048]{1,0:T(8,128)(2,1)} %l_in.1) | copy-start | bytes 589828
  0.9 0.9 %copy-start.1 = (bf16[32,2048]{1,0:T(8,128)(2,1)S(1)}, bf16[32,2048]{1,0:T(8,128)(2,1)}, u32[]{:S(2)}) copy-start(bf16[32,2048]{1,0:T(8,128)(2,1)} %q_in.1) | copy-start | bytes 393220
  1.8 0.7 %copy-start.2 = (s32[2]{0:T(128)S(1)}, s32[2]{0:T(128)}, u32[]{:S(2)}) copy-start(s32[2]{0:T(128)} %w_in.1) | copy-start | bytes 28
  2.5 0.7 %copy-start.3 = (s32[6]{0:T(128)S(1)}, s32[6]{0:T(128)}, u32[]{:S(2)}) copy-start(s32[6]{0:T(128)} %b_in.1) | copy-start | bytes 76
  3.1 0.7 %copy-start.4 = (s32[4]{0:T(128)S(1)}, s32[4]{0:T(128)}, u32[]{:S(2)}) copy-start(s32[4]{0:T(128)} %s_in.1) | copy-start | bytes 52

commit v2 on v1

v2 whole, which is shorter than its diff:
```python
import functools
import math

import jax
import jax.numpy as jnp
from jax import lax
from jax.experimental import pallas as pl
from jax.experimental.pallas import tpu as pltpu
from jax.sharding import PartitionSpec as P

BINS = 2048
NOFF = 4
TOPK = 16
MAXSHIFT = 24
QBLK = 16
LBLK = 8
SPAN = 4
EPS = 1e-06
MASKED = -8.0

QD = 32
LD = 48
CH = 16
NQ = 16 * QD
NL = 16 * LD
PAD = BINS + 2 * MAXSHIFT
WIDE = BINS + 128
MESH = pl.DeviceIdType.MESH

SLOTS = [
    (0, 0), (1, 0), (3, 0), (2, 0),
    (0, 1), (0, 3), (1, 1), (1, 3),
    (3, 1), (3, 3), (2, 1), (2, 3),
    (0, 2), (1, 2), (3, 2), (2, 2),
]


def qslot(a, b):
    return SLOTS.index((a % 4, b % 4))


def lplace(dz, c):
    dz %= 8
    if dz == 0:
        return c
    if dz == 4:
        return 14 + c
    d = min(dz, 8 - dz)
    return 2 + 4 * (d - 1) + 2 * c + (1 if dz > 4 else 0)


def batcher(n):
    pairs = []
    p = 1
    while p < n:
        k = p
        while k >= 1:
            for j in range(k % p, n - k, 2 * k):
                for i in range(min(k, n - j - k)):
                    if (i + j) // (2 * p) == (i + j + k) // (2 * p):
                        pairs.append((i + j, i + j + k))
            k //= 2
        p *= 2
    return pairs


SORT16 = batcher(16)


def sort16(v):
    v = list(v)
    for i, j in SORT16:
        v[i], v[j] = jnp.maximum(v[i], v[j]), jnp.minimum(v[i], v[j])
    return v


def merge16(a, b):
    v = [jnp.maximum(a[i], b[15 - i]) for i in range(16)]
    for d in (8, 4, 2, 1):
        for i in range(16):
            if not i & d:
                v[i], v[i + d] = jnp.maximum(v[i], v[i + d]), jnp.minimum(v[i], v[i + d])
    return v


def kernel(
    q_in, w_hbm, l_in, b_hbm, s_hbm, out,
    w_in, b_in, s_in, qbuf, lbuf, qt32, qtk, sc, lsc, lband, qrow, best, lmeta, fin, got,
    loc_sem, qs_sem, qr_sem, ls_sem, lr_sem, ss_sem, sr_sem, ms_sem, mr_sem, f_sem,
):
    blk = lax.axis_index("blk")
    grp = lax.axis_index("grp")
    core = lax.rem(blk, 2)
    z = lax.rem(lax.div(blk, 2), 8)
    x = lax.div(grp, 2)
    y = lax.rem(grp, 2) * 2 + lax.div(blk, 16)

    def place(px, py, pz, pc):
        return {
            "blk": (lax.rem(py, 2) * 8 + pz) * 2 + pc,
            "grp": px * 2 + lax.div(py, 2),
        }

    def plane(a, b):
        dx = a * (1 - core) + b * core
        dy = b * (1 - core) + a * core
        return place(lax.rem(x + dx, 4), lax.rem(y + dy, 4), z, core)

    def column(dz, dc):
        return place(x, y, lax.rem(z + dz, 8), core + dc * (1 - 2 * core))

    barrier = pltpu.get_barrier_semaphore()
    near = [plane(1, 0), plane(3, 0), plane(0, 1), plane(0, 3)]
    near += [column(1, 0), column(7, 0), column(0, 1)]
    for peer in near:
        pl.semaphore_signal(barrier, inc=1, device_id=peer, device_id_type=MESH)
    loc_q = pltpu.make_async_copy(q_in, qbuf.at[pl.ds(0, QD), pl.ds(0, BINS)], loc_sem.at[0])
    loc_l = pltpu.make_async_copy(l_in, lbuf.at[pl.ds(0, LD)], loc_sem.at[1])
    loc_q.start()
    loc_l.start()
    small = [
        pltpu.make_async_copy(src, dst, loc_sem.at[2 + i])
        for i, (src, dst) in enumerate(((w_hbm, w_in), (b_hbm, b_in), (s_hbm, s_in)))
    ]
    for c in small:
        c.start()
    pl.semaphore_wait(barrier, len(near))

    sends = []

    def lrows(dz, chunk):
        return lbuf.at[pl.ds(LD * lplace(dz, 0) + CH * chunk, CH)]

    def lsem(dz, chunk):
        return ((dz - 1) * 3) + chunk

    def l_send(src, dst_dz, chunk, step):
        n = lsem(dst_dz % 8, chunk)
        c = pltpu.make_async_remote_copy(
            src_ref=src, dst_ref=lrows(dst_dz, chunk), send_sem=ls_sem.at[n],
            recv_sem=lr_sem.at[n], device_id=column(step, 0), device_id_type=MESH,
        )
        c.start()
        sends.append(c)

    def l_wait(dz, chunk):
        n = lsem(dz % 8, chunk)
        ref = lrows(dz, chunk)
        pltpu.make_async_copy(ref, ref, lr_sem.at[n]).wait()

    def l_forward(d, n):
        l_wait(8 - d, n)
        l_wait(d, 2 - n)
        if d < 3:
            l_send(lrows(8 - d, n), 7 - d, n, 1)
            l_send(lrows(d, 2 - n), d + 1, 2 - n, 7)
        elif n == 0:
            l_send(lrows(5, 0), 4, 0, 1)
            l_send(lrows(3, 2), 4, 2, 7)

    def l_middle():
        row = LD * (lplace(5, 0) * (1 - core) + lplace(3, 0) * core) + CH
        src = lbuf.at[pl.ds(pl.multiple_of(row, CH), CH)]
        l_send(src, 4, 1, 1 + 6 * core)

    def m_send(src_dz, dst_dz, step):
        c = pltpu.make_async_remote_copy(
            src_ref=lmeta.at[src_dz], dst_ref=lmeta.at[dst_dz],
            send_sem=ms_sem.at[dst_dz], recv_sem=mr_sem.at[dst_dz],
            device_id=column(step, 0), device_id_type=MESH,
        )
        c.start()
        sends.append(c)

    def m_wait(dz):
        pltpu.make_async_copy(lmeta.at[dz], lmeta.at[dz], mr_sem.at[dz]).wait()

    def m_forward(d):
        m_wait(8 - d)
        m_wait(d)
        m_send(8 - d, 7 - d, 1)
        if d < 3:
            m_send(d, d + 1, 7)

    def sib(src, dz):
        c = pltpu.make_async_remote_copy(
            src_ref=src, dst_ref=lbuf.at[pl.ds(LD * lplace(dz, 1), LD)],
            send_sem=ss_sem.at[dz], recv_sem=sr_sem.at[dz],
            device_id=column(0, 1), device_id_type=MESH,
        )
        c.start()
        sends.append(c)

    def sib_forward(dz):
        sib(lbuf.at[pl.ds(LD * lplace(dz, 0), LD)], dz)

    def sib_wait(dz):
        ref = lbuf.at[pl.ds(LD * lplace(dz, 1), LD)]
        pltpu.make_async_copy(ref, ref, sr_sem.at[dz]).wait()

    def qrows(a, b, half=None):
        s = QD * qslot(a, b)
        if half is None:
            return qbuf.at[pl.ds(s, QD)]
        return qbuf.at[pl.ds(s + 16 * half, 16)]

    def qsem(a, b, half):
        return qslot(a, b) * 2 + (half or 0)

    def q_send(src, a, b, half, to):
        n = qsem(a, b, half)
        c = pltpu.make_async_remote_copy(
            src_ref=src, dst_ref=qrows(a, b, half), send_sem=qs_sem.at[n],
            recv_sem=qr_sem.at[n], device_id=plane(*to), device_id_type=MESH,
        )
        c.start()
        sends.append(c)

    def q_wait(a, b, half=None):
        ref = qrows(a, b, half)
        pltpu.make_async_copy(ref, ref, qr_sem.at[qsem(a, b, half)]).wait()

    for n in range(3):
        l_send(l_in.at[pl.ds(CH * n, CH)], 7, n, 1)
        l_send(l_in.at[pl.ds(CH * (2 - n), CH)], 1, 2 - n, 7)
    sib(l_in, 0)

    lane = lax.broadcasted_iota(jnp.int32, (1, 128), 1)

    def squares(ref, rows):
        acc = jnp.zeros((rows, 128), jnp.float32)
        for t in range(BINS // 128):
            v = ref[0:rows, 128 * t:128 * (t + 1)].astype(jnp.float32)
            acc = acc + v * v
        return acc

    for c in small:
        c.wait()
    loc_q.wait()
    total = jnp.sum(squares(qbuf, QD), axis=1, keepdims=True)
    qscale = lax.rsqrt(total * (1.0 / BINS) + EPS) * (1.0 / math.sqrt(BINS))
    high = qscale.astype(jnp.bfloat16).astype(jnp.float32)
    mid = (qscale - high).astype(jnp.bfloat16).astype(jnp.float32)
    rest = qscale - high - mid
    row = lax.broadcasted_iota(jnp.int32, (QD, 128), 0)
    col = lax.broadcasted_iota(jnp.int32, (QD, 128), 1)
    ext = jnp.where(row < QBLK, w_in[0], w_in[1]).astype(jnp.float32)
    for i, piece in enumerate((high, mid, rest)):
        ext = jnp.where(col == i + 1, piece, ext)
    qbuf[0:QD, BINS:WIDE] = ext.astype(jnp.bfloat16)
    q_send(qrows(0, 0), 3, 0, None, (1, 0))
    q_send(qrows(0, 0), 1, 0, None, (3, 0))

    loc_l.wait()
    acc = squares(lbuf, LD)
    acc = jnp.concatenate([acc, jnp.zeros((128 - LD, 128), jnp.float32)], axis=0)
    total = jnp.sum(acc.T, axis=0, keepdims=True)
    lscale = lax.rsqrt(total * (1.0 / BINS) + EPS)
    row_band = jnp.zeros((1, 128), jnp.int32)
    for j in range(LD // LBLK):
        row_band = jnp.where(lane >= 64 + LBLK * j, b_in[j], row_band)
    lmeta[0] = jnp.where(lane < 64, lscale, row_band.astype(jnp.float32))
    m_send(0, 7, 1)
    m_send(0, 1, 7)
    q_send(qrows(0, 0), 0, 3, None, (0, 1))
    q_send(qrows(0, 0), 0, 1, None, (0, 3))

    qt32[:, 0:MAXSHIFT, :] = jnp.zeros((4, MAXSHIFT, 128), jnp.float32)
    qt32[:, BINS + MAXSHIFT:PAD, :] = jnp.zeros((4, MAXSHIFT, 128), jnp.float32)
    best[...] = jnp.full(best.shape, -jnp.inf, jnp.float32)

    eye_r = lax.broadcasted_iota(jnp.int32, (256, 256), 0)
    eye_c = lax.broadcasted_iota(jnp.int32, (256, 256), 1)
    eye = (eye_r == eye_c).astype(jnp.float32).astype(jnp.bfloat16)

    def turned(t, c0, width):
        return lax.dot_general(
            eye[0:width, 0:width], qbuf[128 * t:128 * t + 128, pl.ds(c0, width)],
            (((1,), (1,)), ((), ())), preferred_element_type=jnp.float32,
        )

    def prepare(t):
        cols = slice(128 * t, 128 * t + 128)

        @pl.loop(0, BINS // 256)
        def _(i):
            c0 = pl.multiple_of(i * 256, 256)
            r0 = pl.multiple_of(MAXSHIFT + c0, 8)
            qt32[t, pl.ds(r0, 256), :] = turned(t, c0, 256)

        ext = turned(t, BINS, 128)
        qrow[0:1, cols] = ext[1:2] + ext[2:3] + ext[3:4]
        qrow[1:2, cols] = ext[0:1]
        for k in range(NOFF):
            off = s_in[k] + MAXSHIFT

            @pl.loop(0, BINS // 256)
            def _(i):
                r0 = pl.multiple_of(i * 256, 256)
                v = qt32[t, pl.ds(r0 + off, 256), :]
                qtk[k, pl.ds(r0, 256), cols] = v.astype(jnp.bfloat16)

    def multiply(row, rows, h):
        cols = slice(256 * h, 256 * h + 256)
        for k in range(NOFF):
            d = jnp.dot(
                lbuf[row:row + rows, :], qtk[k, :, cols], preferred_element_type=jnp.float32
            )
            if k:
                d = jnp.maximum(sc[row:row + rows, cols], d)
            sc[row:row + rows, cols] = d

    def select(g0, g1, tiles):
        @pl.loop(g0, g1)
        def _(g):
            for t in tiles:
                cols = slice(128 * t, 128 * t + 128)
                scale_q = jnp.broadcast_to(qrow[0:1, cols], (8, 128))
                low = jnp.broadcast_to(qrow[1:2, cols], (8, 128))
                high = low + float(SPAN)
                vals = []
                for i in range(16):
                    r = pl.multiple_of(g * 128 + 8 * i, 8)
                    band = lband[pl.ds(r, 8), :]
                    v = sc[pl.ds(r, 8), cols] * scale_q * lsc[pl.ds(r, 8), :]
                    keep = (band >= low) & (band < high)
                    vals.append(jnp.where(keep, v, MASKED))
                vals = sort16(vals)
                vals = merge16([best[t, i] for i in range(16)], vals)
                for i in range(16):
                    best[t, i] = vals[i]

    def q_far(a):
        q_wait(a, 1)
        q_wait(a, 3)
        q_send(qrows(a, 1, 1), a, 2, 1, (0, 3))
        q_send(qrows(a, 3, 0), a, 2, 0, (0, 1))

    l_forward(1, 0)
    q_wait(1, 0)
    q_wait(3, 0)
    q_send(qrows(1, 0, 1), 2, 0, 1, (3, 0))
    q_send(qrows(3, 0, 0), 2, 0, 0, (1, 0))
    for a in (1, 3):
        q_send(qrows(a, 0), a, 3, None, (0, 1))
        q_send(qrows(a, 0), a, 1, None, (0, 3))
    m_forward(1)
    l_forward(1, 1)
    q_far(0)
    q_wait(2, 0, 0)
    q_wait(2, 0, 1)
    q_send(qrows(2, 0), 2, 3, None, (0, 1))
    q_send(qrows(2, 0), 2, 1, None, (0, 3))
    prepare(0)
    m_forward(2)
    l_forward(1, 2)
    sib_forward(1)
    sib_forward(7)
    q_far(1)
    l_forward(2, 0)
    prepare(1)
    m_forward(3)
    for dz in (0, 1, 7):
        sib_wait(dz)
    multiply(0, 288, 0)
    l_forward(2, 1)
    q_far(3)
    q_far(2)
    l_forward(2, 2)
    sib_forward(2)
    sib_forward(6)

    m_wait(4)
    pltpu.make_async_remote_copy(
        src_ref=lmeta.at[pl.ds(0, 8)], dst_ref=lmeta.at[pl.ds(8, 8)], send_sem=ms_sem.at[0],
        recv_sem=mr_sem.at[0], device_id=column(0, 1), device_id_type=MESH,
    ).start()
    prepare(2)
    l_forward(3, 0)
    sib_wait(2)
    sib_wait(6)
    multiply(288, 192, 0)
    pltpu.make_async_copy(lmeta.at[pl.ds(8, 8)], lmeta.at[pl.ds(8, 8)], mr_sem.at[0]).wait()
    for c in range(2):
        for dz in range(8):
            m = jnp.broadcast_to(lmeta[8 * c + dz], (128, 128)).T
            r = LD * lplace(dz, c)
            lsc[r:r + LD, :] = m[0:LD]
            lband[r:r + LD, :] = m[64:64 + LD]
    l_wait(5, 1)
    l_wait(3, 1)
    l_middle()
    for a in (0, 1, 3, 2):
        q_wait(a, 2, 0)
        q_wait(a, 2, 1)
    prepare(3)
    multiply(0, 288, 1)
    l_wait(5, 2)
    l_wait(3, 0)
    sib_forward(3)
    sib_forward(5)
    multiply(288, 192, 1)
    for n in range(3):
        l_wait(4, n)
    sib_forward(4)
    select(0, 3, range(4))
    sib_wait(3)
    sib_wait(5)
    multiply(480, 192, 0)
    multiply(480, 192, 1)
    select(3, 5, range(4))
    sib_wait(4)

    def finish(t):
        vals = [best[t, i] for i in range(16)]
        for sh in (4, 2, 1):
            vals = merge16(vals, [pltpu.roll(v, sh, 0) for v in vals])
        for i in range(16):
            fin[t, i:i + 1, :] = vals[i][0:1]
        for p in (3, 2, 1, 0):
            n = 4 * t + p
            if n == 0:
                continue
            a, b = SLOTS[n]
            pltpu.make_async_remote_copy(
                src_ref=fin.at[t], dst_ref=got.at[n], send_sem=f_sem.at[0],
                recv_sem=f_sem.at[1], device_id=plane(a, b), device_id_type=MESH,
            ).start()

    for h in (1, 0):
        multiply(672, 96, h)
        for t in (2 * h + 1, 2 * h):
            select(5, 6, (t,))
            finish(t)
    got[0] = fin[0]
    for c in sends:
        c.wait_send()
    pltpu.make_async_copy(lmeta.at[pl.ds(0, 8)], lmeta.at[pl.ds(0, 8)], ms_sem.at[0]).wait()
    pltpu.make_async_copy(got.at[pl.ds(1, 15)], got.at[pl.ds(1, 15)], f_sem.at[0]).wait()
    pltpu.make_async_copy(got.at[pl.ds(1, 15)], got.at[pl.ds(1, 15)], f_sem.at[1]).wait()

    part = lax.div(lax.broadcasted_iota(jnp.int32, (8, 128), 1), QD)
    vals = []
    for r in range(16):
        rows = []
        for t in range(4):
            v = got[4 * t, r:r + 1, :]
            for p in range(1, 4):
                v = jnp.where(part[0:1] == p, got[4 * t + p, r:r + 1, :], v)
            rows.append(v)
        vals.append(jnp.concatenate(rows + rows, axis=0))
    for sh in (2, 1):
        vals = merge16(vals, [pltpu.roll(v, sh, 0) for v in vals])
    for sh in (64, 32):
        vals = merge16(vals, [pltpu.roll(v, sh, 1) for v in vals])
    for i in range(TOPK):
        out[i:i + 1, :] = vals[i][0:1, 0:QD]


def local(queries, windows, library, bands, shifts):
    dma = pltpu.SemaphoreType.DMA
    f32, bf16 = jnp.float32, jnp.bfloat16
    hbm = pl.BlockSpec(memory_space=pltpu.HBM)
    return pl.pallas_call(
        kernel,
        out_shape=jax.ShapeDtypeStruct((TOPK, QD), f32),
        in_specs=[hbm] * 5,
        out_specs=pl.BlockSpec(memory_space=pltpu.VMEM),
        scratch_shapes=[
            pltpu.SMEM((2,), jnp.int32),
            pltpu.SMEM((6,), jnp.int32),
            pltpu.SMEM((NOFF,), jnp.int32),
            pltpu.VMEM((NQ, WIDE), bf16),
            pltpu.VMEM((NL, BINS), bf16),
            pltpu.VMEM((4, PAD, 128), f32),
            pltpu.VMEM((NOFF, BINS, NQ), bf16),
            pltpu.VMEM((NL, NQ), f32),
            pltpu.VMEM((NL, 128), f32),
            pltpu.VMEM((NL, 128), f32),
            pltpu.VMEM((8, NQ), f32),
            pltpu.VMEM((4, 16, 8, 128), f32),
            pltpu.VMEM((16, 1, 128), f32),
            pltpu.VMEM((4, 16, 128), f32),
            pltpu.VMEM((16, 16, 128), f32),
            dma((5,)), dma((32,)), dma((32,)), dma((21,)), dma((21,)),
            dma((8,)), dma((8,)), dma((8,)), dma((8,)), dma((2,)),
        ],
        compiler_params=pltpu.CompilerParams(
            collective_id=0, has_side_effects=True, vmem_limit_bytes=62 * 2**20
        ),
        cost_estimate=pl.CostEstimate(
            flops=2 * NQ * NL * BINS * NOFF, bytes_accessed=2 * (QD + LD) * BINS, transcendentals=0
        ),
    )(queries, windows, library, bands, shifts).T


def solution(mesh):
    return jax.shard_map(
        local,
        mesh=mesh,
        in_specs=(
            P(("blk", "grp"), None),
            P(("blk", "grp")),
            P(("blk", "grp"), None),
            P(("blk", "grp")),
            P(),
        ),
        out_specs=P(("blk", "grp"), None),
        check_vma=False,
    )
```

time: 48.6 us -> 47.4 us (0.975)
  local copies, waits for them, and re-layouts: 4.46 us -> 1.3 us
  Pallas kernels: 44 us -> 46 us
    unnamed x10 -> x1, local copies, waits for them, and re-layouts: 3.79 us -> 1.3 us
    pallas_call x1, Pallas kernels: 44 us -> 46 us  [local(): pl.pallas_call(kernel, out_shape=jax.ShapeDtypeStruct((TOPK, QD), f32), i...]
    pallas_call x1 -> x0, local copies, waits for them, and re-layouts: 0.67 us -> none  [local(): pl.pallas_call(kernel, out_shape=jax.ShapeDtypeStruct((QD, TOPK), f32), i...]
where the time goes in v2:
time: 47.4 us; the launch traced here: 47.3 us
  Pallas kernels  46 us (97%)
  local copies, waits for them, and re-layouts  1.3 us (3%)
    pallas_call x1, Pallas kernels, local(): pl.pallas_call(kernel, out_shape=jax.ShapeDtypeStruct((TOPK, QD), f32), i...  46 us
    unnamed x1, local copies, waits for them, and re-layouts  1.3 us

profile of v2, /device:TPU:1, one launch (start us, length us, event | category | flops | bytes accessed | tf_op | source)
XLA Modules:
  0.0 47.3 jit_solution(13998801064960917484)
XLA Ops:
  0.0 46.0 %shard_map.55 = f32[16,32]{1,0:T(8,128)} custom-call(bf16[32,2048]{1,0:T(8,128)(2,1)} %q_in.1, s32[2]{0:T(128)} %w_hbm.1, bf16[48,2048]{1,0:T(8,128)(2,1)} %l_in.1, s32[6]{0:T(128)} %b_hbm.1, s32[4]{0:T(128)} %s_hbm.1), custom_call_target="tpu_custom_call" | custom-call | flops 6442450944 | bytes 327680 | tf_op jit(solution)/shard_map/pallas_call | solution.py:464
  46.0 1.3 %copy.7 = f32[32,16]{0,1:T(8,128)} copy(f32[32,16]{0,1:T(8,128)} %bitcast.1) | data formatting | bytes 4096

commit v3 on v2

--- a/solution.py
+++ b/solution.py
@@ -198,32 +198,50 @@
         ref = lbuf.at[pl.ds(LD * lplace(dz, 1), LD)]
         pltpu.make_async_copy(ref, ref, sr_sem.at[dz]).wait()
 
-    def qrows(a, b, half=None):
-        s = QD * qslot(a, b)
-        if half is None:
-            return qbuf.at[pl.ds(s, QD)]
-        return qbuf.at[pl.ds(s + 16 * half, 16)]
-
-    def qsem(a, b, half):
-        return qslot(a, b) * 2 + (half or 0)
-
-    def q_send(src, a, b, half, to):
-        n = qsem(a, b, half)
+    def qrows(a, b, half):
+        return qbuf.at[pl.ds(QD * qslot(a, b) + 16 * half, 16)]
+
+    def q_copy(src, dst, n, to):
         c = pltpu.make_async_remote_copy(
-            src_ref=src, dst_ref=qrows(a, b, half), send_sem=qs_sem.at[n],
-            recv_sem=qr_sem.at[n], device_id=plane(*to), device_id_type=MESH,
+            src_ref=src, dst_ref=dst, send_sem=qs_sem.at[n],
+            recv_sem=qr_sem.at[n], device_id=plane(to[0] % 4, to[1] % 4),
+            device_id_type=MESH,
         )
         c.start()
         sends.append(c)
 
-    def q_wait(a, b, half=None):
-        ref = qrows(a, b, half)
-        pltpu.make_async_copy(ref, ref, qr_sem.at[qsem(a, b, half)]).wait()
+    def q_own(a, b, to):
+        for half in range(2):
+            dst = qbuf.at[pl.ds(QD * qslot(a, b) + 16 * half, 16), pl.ds(0, BINS)]
+            q_copy(q_in.at[pl.ds(16 * half, 16)], dst, qslot(a, b) * 2 + half, to)
+
+    EXT = ((1, 0), (3, 0), (0, 1), (0, 3))
+
+    def ext_ref(a, b):
+        return qbuf.at[pl.ds(QD * qslot(a, b), QD), pl.ds(BINS, 128)]
+
+    def q_ext(a, b, to):
+        q_copy(ext_ref(0, 0), ext_ref(a, b), 32 + EXT.index((a, b)), to)
+
+    def ext_wait(a, b):
+        ref = ext_ref(a, b)
+        pltpu.make_async_copy(ref, ref, qr_sem.at[32 + EXT.index((a, b))]).wait()
+
+    def q_send(a, b, half, to):
+        na, nb = a - to[0], b - to[1]
+        q_copy(qrows(a, b, half), qrows(na, nb, half), qslot(na, nb) * 2 + half, to)
+
+    def q_wait(a, b, half):
+        rows = pl.ds(QD * qslot(a, b) + 16 * half, 16)
+        ref = qbuf.at[rows, pl.ds(0, BINS)] if (a, b) in EXT else qbuf.at[rows]
+        pltpu.make_async_copy(ref, ref, qr_sem.at[qslot(a, b) * 2 + half]).wait()
 
     for n in range(3):
         l_send(l_in.at[pl.ds(CH * n, CH)], 7, n, 1)
         l_send(l_in.at[pl.ds(CH * (2 - n), CH)], 1, 2 - n, 7)
     sib(l_in, 0)
+    q_own(3, 0, (1, 0))
+    q_own(1, 0, (3, 0))
 
     lane = lax.broadcasted_iota(jnp.int32, (1, 128), 1)
 
@@ -248,8 +266,10 @@
     for i, piece in enumerate((high, mid, rest)):
         ext = jnp.where(col == i + 1, piece, ext)
     qbuf[0:QD, BINS:WIDE] = ext.astype(jnp.bfloat16)
-    q_send(qrows(0, 0), 3, 0, None, (1, 0))
-    q_send(qrows(0, 0), 1, 0, None, (3, 0))
+    q_ext(3, 0, (1, 0))
+    q_ext(1, 0, (3, 0))
+    q_ext(0, 3, (0, 1))
+    q_ext(0, 1, (0, 3))
 
     loc_l.wait()
     acc = squares(lbuf, LD)
@@ -262,8 +282,8 @@
     lmeta[0] = jnp.where(lane < 64, lscale, row_band.astype(jnp.float32))
     m_send(0, 7, 1)
     m_send(0, 1, 7)
-    q_send(qrows(0, 0), 0, 3, None, (0, 1))
-    q_send(qrows(0, 0), 0, 1, None, (0, 3))
+    q_own(0, 3, (0, 1))
+    q_own(0, 1, (0, 3))
 
     qt32[:, 0:MAXSHIFT, :] = jnp.zeros((4, MAXSHIFT, 128), jnp.float32)
     qt32[:, BINS + MAXSHIFT:PAD, :] = jnp.zeros((4, MAXSHIFT, 128), jnp.float32)
@@ -273,32 +293,31 @@
     eye_c = lax.broadcasted_iota(jnp.int32, (256, 256), 1)
     eye = (eye_r == eye_c).astype(jnp.float32).astype(jnp.bfloat16)
 
-    def turned(t, c0, width):
+    def turned(h, c0, width):
         return lax.dot_general(
-            eye[0:width, 0:width], qbuf[128 * t:128 * t + 128, pl.ds(c0, width)],
+            eye[0:width, 0:width], qbuf[256 * h:256 * h + 256, c0:c0 + width],
             (((1,), (1,)), ((), ())), preferred_element_type=jnp.float32,
         )
 
-    def prepare(t):
-        cols = slice(128 * t, 128 * t + 128)
-
-        @pl.loop(0, BINS // 256)
-        def _(i):
-            c0 = pl.multiple_of(i * 256, 256)
-            r0 = pl.multiple_of(MAXSHIFT + c0, 8)
-            qt32[t, pl.ds(r0, 256), :] = turned(t, c0, 256)
-
-        ext = turned(t, BINS, 128)
+    def prepare(h):
+        cols = slice(256 * h, 256 * h + 256)
+        for c0 in range(0, BINS, 256):
+            v = turned(h, c0, 256)
+            r0 = MAXSHIFT + c0
+            qt32[2 * h, r0:r0 + 256, :] = v[:, 0:128]
+            qt32[2 * h + 1, r0:r0 + 256, :] = v[:, 128:256]
+        ext = turned(h, BINS, 128)
         qrow[0:1, cols] = ext[1:2] + ext[2:3] + ext[3:4]
         qrow[1:2, cols] = ext[0:1]
-        for k in range(NOFF):
-            off = s_in[k] + MAXSHIFT
-
-            @pl.loop(0, BINS // 256)
-            def _(i):
-                r0 = pl.multiple_of(i * 256, 256)
-                v = qt32[t, pl.ds(r0 + off, 256), :]
-                qtk[k, pl.ds(r0, 256), cols] = v.astype(jnp.bfloat16)
+        offs = [s_in[k] + MAXSHIFT for k in range(NOFF)]
+
+        @pl.loop(0, BINS // 128)
+        def _(i):
+            r0 = pl.multiple_of(i * 128, 128)
+            for k in range(NOFF):
+                for t in (2 * h, 2 * h + 1):
+                    v = qt32[t, pl.ds(r0 + offs[k], 128), :]
+                    qtk[k, pl.ds(r0, 128), 128 * t:128 * t + 128] = v.astype(jnp.bfloat16)
 
     def multiply(row, rows, h):
         cols = slice(256 * h, 256 * h + 256)
@@ -330,56 +349,91 @@
                 for i in range(16):
                     best[t, i] = vals[i]
 
-    def q_far(a):
-        q_wait(a, 1)
-        q_wait(a, 3)
-        q_send(qrows(a, 1, 1), a, 2, 1, (0, 3))
-        q_send(qrows(a, 3, 0), a, 2, 0, (0, 1))
-
+    def q_first(a, half):
+        if half == (1 if a == 1 else 0):
+            ext_wait(a, 0)
+        q_wait(a, 0, half)
+        if (a, half) == (1, 1):
+            q_send(1, 0, 1, (-1, 0))
+        if (a, half) == (3, 0):
+            q_send(3, 0, 0, (1, 0))
+        q_send(a, 0, half, (0, 1))
+        q_send(a, 0, half, (0, -1))
+
+    def q_across(half):
+        q_wait(2, 0, half)
+        q_send(2, 0, half, (0, 1))
+        q_send(2, 0, half, (0, -1))
+
+    def q_second(a, half):
+        b = 1 if half else 3
+        if a == 0:
+            ext_wait(0, b)
+        q_wait(a, b, half)
+        q_send(a, b, half, (0, -1) if half else (0, 1))
+
+    def q_rest(a):
+        q_wait(a, 1, 0)
+        q_wait(a, 3, 1)
+
+    q_first(3, 0)
+    q_first(1, 1)
     l_forward(1, 0)
-    q_wait(1, 0)
-    q_wait(3, 0)
-    q_send(qrows(1, 0, 1), 2, 0, 1, (3, 0))
-    q_send(qrows(3, 0, 0), 2, 0, 0, (1, 0))
-    for a in (1, 3):
-        q_send(qrows(a, 0), a, 3, None, (0, 1))
-        q_send(qrows(a, 0), a, 1, None, (0, 3))
+    l_forward(1, 1)
+    q_first(1, 0)
+    q_first(3, 1)
     m_forward(1)
-    l_forward(1, 1)
-    q_far(0)
-    q_wait(2, 0, 0)
-    q_wait(2, 0, 1)
-    q_send(qrows(2, 0), 2, 3, None, (0, 1))
-    q_send(qrows(2, 0), 2, 1, None, (0, 3))
+    l_forward(1, 2)
+    q_across(0)
+    q_second(0, 0)
+    q_across(1)
+    q_second(3, 0)
+    sib_forward(1)
+    sib_forward(7)
+    q_second(1, 1)
+    l_forward(2, 0)
+    q_second(0, 1)
+    q_rest(0)
+    q_rest(1)
+    q_second(1, 0)
     prepare(0)
     m_forward(2)
-    l_forward(1, 2)
-    sib_forward(1)
-    sib_forward(7)
-    q_far(1)
-    l_forward(2, 0)
-    prepare(1)
-    m_forward(3)
+    l_forward(2, 1)
+    q_second(2, 0)
+    q_second(3, 1)
+    l_forward(2, 2)
+    sib_forward(2)
+    sib_forward(6)
+    q_second(2, 1)
     for dz in (0, 1, 7):
         sib_wait(dz)
     multiply(0, 288, 0)
-    l_forward(2, 1)
-    q_far(3)
-    q_far(2)
-    l_forward(2, 2)
-    sib_forward(2)
-    sib_forward(6)
-
+    sib_wait(2)
+    sib_wait(6)
+    multiply(288, 192, 0)
+    l_forward(3, 0)
+    l_wait(5, 1)
+    l_wait(3, 1)
+    l_middle()
+    m_forward(3)
+    q_rest(3)
+    q_rest(2)
+    for a in range(4):
+        q_wait(a, 2, 0)
+        q_wait(a, 2, 1)
+    prepare(1)
+    l_wait(5, 2)
+    l_wait(3, 0)
+    sib_forward(3)
+    sib_forward(5)
+    multiply(0, 288, 1)
     m_wait(4)
     pltpu.make_async_remote_copy(
         src_ref=lmeta.at[pl.ds(0, 8)], dst_ref=lmeta.at[pl.ds(8, 8)], send_sem=ms_sem.at[0],
         recv_sem=mr_sem.at[0], device_id=column(0, 1), device_id_type=MESH,
     ).start()
-    prepare(2)
-    l_forward(3, 0)
-    sib_wait(2)
-    sib_wait(6)
-    multiply(288, 192, 0)
+    multiply(288, 192, 1)
+
     pltpu.make_async_copy(lmeta.at[pl.ds(8, 8)], lmeta.at[pl.ds(8, 8)], mr_sem.at[0]).wait()
     for c in range(2):
         for dz in range(8):
@@ -387,28 +441,13 @@
             r = LD * lplace(dz, c)
             lsc[r:r + LD, :] = m[0:LD]
             lband[r:r + LD, :] = m[64:64 + LD]
-    l_wait(5, 1)
-    l_wait(3, 1)
-    l_middle()
-    for a in (0, 1, 3, 2):
-        q_wait(a, 2, 0)
-        q_wait(a, 2, 1)
-    prepare(3)
-    multiply(0, 288, 1)
-    l_wait(5, 2)
-    l_wait(3, 0)
-    sib_forward(3)
-    sib_forward(5)
-    multiply(288, 192, 1)
     for n in range(3):
         l_wait(4, n)
     sib_forward(4)
-    select(0, 3, range(4))
     sib_wait(3)
     sib_wait(5)
-    multiply(480, 192, 0)
     multiply(480, 192, 1)
-    select(3, 5, range(4))
+    select(0, 5, (2, 3))
     sib_wait(4)
 
     def finish(t):
@@ -428,6 +467,9 @@
             ).start()
 
     for h in (1, 0):
+        if h == 0:
+            multiply(480, 192, 0)
+            select(0, 5, (0, 1))
         multiply(672, 96, h)
         for t in (2 * h + 1, 2 * h):
             select(5, 6, (t,))
@@ -482,7 +524,7 @@
             pltpu.VMEM((16, 1, 128), f32),
             pltpu.VMEM((4, 16, 128), f32),
             pltpu.VMEM((16, 16, 128), f32),
-            dma((5,)), dma((32,)), dma((32,)), dma((21,)), dma((21,)),
+            dma((5,)), dma((36,)), dma((36,)), dma((21,)), dma((21,)),
             dma((8,)), dma((8,)), dma((8,)), dma((8,)), dma((2,)),
         ],
         compiler_params=pltpu.CompilerParams(

time: 47.4 us -> 43.8 us (0.924)
  Pallas kernels: 46 us -> 42.3 us
    pallas_call x1, Pallas kernels: 46 us -> 42.3 us  [local(): pl.pallas_call(kernel, out_shape=jax.ShapeDtypeStruct((TOPK, QD), f32), i...]
where the time goes in v3:
time: 43.8 us; the launch traced here: 43.6 us
  Pallas kernels  42.3 us (97%)
  local copies, waits for them, and re-layouts  1.3 us (3%)
    pallas_call x1, Pallas kernels, local(): pl.pallas_call(kernel, out_shape=jax.ShapeDtypeStruct((TOPK, QD), f32), i...  42.3 us
    unnamed x1, local copies, waits for them, and re-layouts  1.3 us

profile of v3, /device:TPU:1, one launch (start us, length us, event | category | flops | bytes accessed | tf_op | source)
XLA Modules:
  0.0 43.6 jit_solution(12821611574713041386)
XLA Ops:
  0.0 42.3 %shard_map.55 = f32[16,32]{1,0:T(8,128)} custom-call(bf16[32,2048]{1,0:T(8,128)(2,1)} %q_in.1, s32[2]{0:T(128)} %w_hbm.1, bf16[48,2048]{1,0:T(8,128)(2,1)} %l_in.1, s32[6]{0:T(128)} %b_hbm.1, s32[4]{0:T(128)} %s_hbm.1), custom_call_target="tpu_custom_call" | custom-call | flops 6442450944 | bytes 327680 | tf_op jit(solution)/shard_map/pallas_call | solution.py:506
  42.3 1.3 %copy.7 = f32[32,16]{0,1:T(8,128)} copy(f32[32,16]{0,1:T(8,128)} %bitcast.1) | data formatting | bytes 4096

commit v4 on v3

--- a/solution.py
+++ b/solution.py
@@ -128,40 +128,47 @@
 
     sends = []
 
-    def lrows(dz, chunk):
-        return lbuf.at[pl.ds(LD * lplace(dz, 0) + CH * chunk, CH)]
-
-    def lsem(dz, chunk):
-        return ((dz - 1) * 3) + chunk
-
-    def l_send(src, dst_dz, chunk, step):
-        n = lsem(dst_dz % 8, chunk)
+    UP = ((0, 32), (32, 16))
+    DOWN = ((16, 32), (0, 16))
+
+    def lrows(dz, part):
+        if dz == 4:
+            return lbuf.at[pl.ds(LD * lplace(4, 0), LD)]
+        r, n = (UP if dz > 4 else DOWN)[part]
+        return lbuf.at[pl.ds(LD * lplace(dz, 0) + r, n)]
+
+    def l_copy(src, dst, n_send, n_recv, step):
         c = pltpu.make_async_remote_copy(
-            src_ref=src, dst_ref=lrows(dst_dz, chunk), send_sem=ls_sem.at[n],
-            recv_sem=lr_sem.at[n], device_id=column(step, 0), device_id_type=MESH,
+            src_ref=src, dst_ref=dst, send_sem=ls_sem.at[n_send],
+            recv_sem=lr_sem.at[n_recv], device_id=column(step, 0), device_id_type=MESH,
         )
         c.start()
         sends.append(c)
 
-    def l_wait(dz, chunk):
-        n = lsem(dz % 8, chunk)
-        ref = lrows(dz, chunk)
-        pltpu.make_async_copy(ref, ref, lr_sem.at[n]).wait()
-
-    def l_forward(d, n):
-        l_wait(8 - d, n)
-        l_wait(d, 2 - n)
-        if d < 3:
-            l_send(lrows(8 - d, n), 7 - d, n, 1)
-            l_send(lrows(d, 2 - n), d + 1, 2 - n, 7)
-        elif n == 0:
-            l_send(lrows(5, 0), 4, 0, 1)
-            l_send(lrows(3, 2), 4, 2, 7)
-
-    def l_middle():
-        row = LD * (lplace(5, 0) * (1 - core) + lplace(3, 0) * core) + CH
-        src = lbuf.at[pl.ds(pl.multiple_of(row, CH), CH)]
-        l_send(src, 4, 1, 1 + 6 * core)
+    def l_send(src, dz, part, step):
+        n = 2 * dz + part
+        l_copy(src, lrows(dz, part), n, n, step)
+
+    def l_wait(dz, part):
+        ref = lrows(dz, part)
+        pltpu.make_async_copy(ref, ref, lr_sem.at[2 * dz + part]).wait()
+
+    def l_forward(d, part):
+        l_wait(8 - d, part)
+        l_wait(d, part)
+        l_send(lrows(8 - d, part), 7 - d, part, 1)
+        l_send(lrows(d, part), d + 1, part, 7)
+
+    def l_last():
+        l_wait(5, 0)
+        l_wait(3, 0)
+        up, down, far = (LD * lplace(dz, 0) for dz in (5, 3, 4))
+        mid = up * (1 - core) + down * core + CH
+        for i, (src, r, step) in enumerate(
+            ((up, 0, 1), (down + 2 * CH, 2 * CH, 7), (mid, CH, 1 + 6 * core))
+        ):
+            src = lbuf.at[pl.ds(pl.multiple_of(src, CH), CH)]
+            l_copy(src, lbuf.at[pl.ds(far + r, CH)], (8, 9, 0)[i], 8, step)
 
     def m_send(src_dz, dst_dz, step):
         c = pltpu.make_async_remote_copy(
@@ -182,29 +189,33 @@
         if d < 3:
             m_send(d, d + 1, 7)
 
-    def sib(src, dz):
+    def sib(src, d):
+        rows = src.shape[0]
         c = pltpu.make_async_remote_copy(
-            src_ref=src, dst_ref=lbuf.at[pl.ds(LD * lplace(dz, 1), LD)],
-            send_sem=ss_sem.at[dz], recv_sem=sr_sem.at[dz],
+            src_ref=src, dst_ref=lbuf.at[pl.ds(LD * lplace(d, 1), rows)],
+            send_sem=ss_sem.at[d], recv_sem=sr_sem.at[d],
             device_id=column(0, 1), device_id_type=MESH,
         )
         c.start()
         sends.append(c)
 
-    def sib_forward(dz):
-        sib(lbuf.at[pl.ds(LD * lplace(dz, 0), LD)], dz)
-
-    def sib_wait(dz):
-        ref = lbuf.at[pl.ds(LD * lplace(dz, 1), LD)]
-        pltpu.make_async_copy(ref, ref, sr_sem.at[dz]).wait()
+    def sib_forward(d):
+        sib(lbuf.at[pl.ds(LD * lplace(d, 0), LD if d == 4 else 2 * LD)], d)
+
+    def sib_wait(d):
+        ref = lbuf.at[pl.ds(LD * lplace(d, 1), 2 * LD if d in (1, 2, 3) else LD)]
+        pltpu.make_async_copy(ref, ref, sr_sem.at[d]).wait()
 
     def qrows(a, b, half):
         return qbuf.at[pl.ds(QD * qslot(a, b) + 16 * half, 16)]
 
-    def q_copy(src, dst, n, to):
+    def is_last(a, b, half):
+        return b == 2 or (a, b, half) in ((3, 1, 0), (3, 3, 1), (2, 1, 0), (2, 3, 1))
+
+    def q_copy(src, dst, n, to, last=False):
         c = pltpu.make_async_remote_copy(
             src_ref=src, dst_ref=dst, send_sem=qs_sem.at[n],
-            recv_sem=qr_sem.at[n], device_id=plane(to[0] % 4, to[1] % 4),
+            recv_sem=qr_sem.at[36 if last else n], device_id=plane(to[0] % 4, to[1] % 4),
             device_id_type=MESH,
         )
         c.start()
@@ -228,17 +239,18 @@
         pltpu.make_async_copy(ref, ref, qr_sem.at[32 + EXT.index((a, b))]).wait()
 
     def q_send(a, b, half, to):
-        na, nb = a - to[0], b - to[1]
-        q_copy(qrows(a, b, half), qrows(na, nb, half), qslot(na, nb) * 2 + half, to)
+        na, nb = (a - to[0]) % 4, (b - to[1]) % 4
+        n = qslot(na, nb) * 2 + half
+        q_copy(qrows(a, b, half), qrows(na, nb, half), n, to, is_last(na, nb, half))
 
     def q_wait(a, b, half):
         rows = pl.ds(QD * qslot(a, b) + 16 * half, 16)
         ref = qbuf.at[rows, pl.ds(0, BINS)] if (a, b) in EXT else qbuf.at[rows]
         pltpu.make_async_copy(ref, ref, qr_sem.at[qslot(a, b) * 2 + half]).wait()
 
-    for n in range(3):
-        l_send(l_in.at[pl.ds(CH * n, CH)], 7, n, 1)
-        l_send(l_in.at[pl.ds(CH * (2 - n), CH)], 1, 2 - n, 7)
+    for part in range(2):
+        l_send(l_in.at[pl.ds(*UP[part])], 7, part, 1)
+        l_send(l_in.at[pl.ds(*DOWN[part])], 1, part, 7)
     sib(l_in, 0)
     q_own(3, 0, (1, 0))
     q_own(1, 0, (3, 0))
@@ -287,7 +299,6 @@
 
     qt32[:, 0:MAXSHIFT, :] = jnp.zeros((4, MAXSHIFT, 128), jnp.float32)
     qt32[:, BINS + MAXSHIFT:PAD, :] = jnp.zeros((4, MAXSHIFT, 128), jnp.float32)
-    best[...] = jnp.full(best.shape, -jnp.inf, jnp.float32)
 
     eye_r = lax.broadcasted_iota(jnp.int32, (256, 256), 0)
     eye_c = lax.broadcasted_iota(jnp.int32, (256, 256), 1)
@@ -319,7 +330,9 @@
                     v = qt32[t, pl.ds(r0 + offs[k], 128), :]
                     qtk[k, pl.ds(r0, 128), 128 * t:128 * t + 128] = v.astype(jnp.bfloat16)
 
-    def multiply(row, rows, h):
+    def multiply(row, rows, h, beside=()):
+        beside = list(beside)
+        each = -(-len(beside) // NOFF)
         cols = slice(256 * h, 256 * h + 256)
         for k in range(NOFF):
             d = jnp.dot(
@@ -328,29 +341,38 @@
             if k:
                 d = jnp.maximum(sc[row:row + rows, cols], d)
             sc[row:row + rows, cols] = d
-
-    def select(g0, g1, tiles):
-        @pl.loop(g0, g1)
-        def _(g):
-            for t in tiles:
-                cols = slice(128 * t, 128 * t + 128)
-                scale_q = jnp.broadcast_to(qrow[0:1, cols], (8, 128))
-                low = jnp.broadcast_to(qrow[1:2, cols], (8, 128))
-                high = low + float(SPAN)
-                vals = []
-                for i in range(16):
-                    r = pl.multiple_of(g * 128 + 8 * i, 8)
-                    band = lband[pl.ds(r, 8), :]
-                    v = sc[pl.ds(r, 8), cols] * scale_q * lsc[pl.ds(r, 8), :]
-                    keep = (band >= low) & (band < high)
-                    vals.append(jnp.where(keep, v, MASKED))
-                vals = sort16(vals)
-                vals = merge16([best[t, i] for i in range(16)], vals)
-                for i in range(16):
-                    best[t, i] = vals[i]
+            for f in beside[each * k:each * (k + 1)]:
+                f()
+
+    def select(g, t):
+        cols = slice(128 * t, 128 * t + 128)
+        scale_q = jnp.broadcast_to(qrow[0:1, cols], (8, 128))
+        low = jnp.broadcast_to(qrow[1:2, cols], (8, 128))
+        high = low + float(SPAN)
+        vals = []
+        for i in range(16):
+            r = g * 128 + 8 * i
+            band = lband[r:r + 8, :]
+            v = sc[r:r + 8, cols] * scale_q * lsc[r:r + 8, :]
+            keep = (band >= low) & (band < high)
+            vals.append(jnp.where(keep, v, MASKED))
+        vals = sort16(vals)
+        if g:
+            vals = merge16([best[t, i] for i in range(16)], vals)
+        for i in range(16):
+            best[t, i] = vals[i]
+
+    def selects(groups, tiles):
+        return [functools.partial(select, g, t) for g in groups for t in tiles]
+
+    def spread(c, dz):
+        m = jnp.broadcast_to(lmeta[8 * c + dz], (128, 128)).T
+        r = LD * lplace(dz, c)
+        lsc[r:r + LD, :] = m[0:LD]
+        lband[r:r + LD, :] = m[64:64 + LD]
 
     def q_first(a, half):
-        if half == (1 if a == 1 else 0):
+        if half == 0:
             ext_wait(a, 0)
         q_wait(a, 0, half)
         if (a, half) == (1, 1):
@@ -376,78 +398,56 @@
         q_wait(a, 1, 0)
         q_wait(a, 3, 1)
 
+    q_first(1, 0)
     q_first(3, 0)
+    l_forward(1, 0)
     q_first(1, 1)
-    l_forward(1, 0)
+    m_forward(1)
     l_forward(1, 1)
-    q_first(1, 0)
+    q_second(0, 1)
     q_first(3, 1)
-    m_forward(1)
-    l_forward(1, 2)
     q_across(0)
+    sib_forward(1)
+    q_second(3, 0)
     q_second(0, 0)
+    q_second(1, 0)
     q_across(1)
-    q_second(3, 0)
-    sib_forward(1)
-    sib_forward(7)
     q_second(1, 1)
+    m_forward(2)
     l_forward(2, 0)
-    q_second(0, 1)
     q_rest(0)
     q_rest(1)
-    q_second(1, 0)
     prepare(0)
-    m_forward(2)
+    q_second(3, 1)
     l_forward(2, 1)
     q_second(2, 0)
-    q_second(3, 1)
-    l_forward(2, 2)
     sib_forward(2)
-    sib_forward(6)
+    m_forward(3)
     q_second(2, 1)
-    for dz in (0, 1, 7):
-        sib_wait(dz)
+    sib_wait(0)
+    sib_wait(1)
     multiply(0, 288, 0)
     sib_wait(2)
-    sib_wait(6)
     multiply(288, 192, 0)
-    l_forward(3, 0)
-    l_wait(5, 1)
-    l_wait(3, 1)
-    l_middle()
-    m_forward(3)
-    q_rest(3)
-    q_rest(2)
-    for a in range(4):
-        q_wait(a, 2, 0)
-        q_wait(a, 2, 1)
+    l_last()
+    ref = qbuf.at[pl.ds(0, 192)]
+    pltpu.make_async_copy(ref, ref, qr_sem.at[36]).wait()
     prepare(1)
-    l_wait(5, 2)
-    l_wait(3, 0)
-    sib_forward(3)
-    sib_forward(5)
-    multiply(0, 288, 1)
     m_wait(4)
     pltpu.make_async_remote_copy(
         src_ref=lmeta.at[pl.ds(0, 8)], dst_ref=lmeta.at[pl.ds(8, 8)], send_sem=ms_sem.at[0],
         recv_sem=mr_sem.at[0], device_id=column(0, 1), device_id_type=MESH,
     ).start()
-    multiply(288, 192, 1)
-
+    multiply(0, 288, 1, [functools.partial(spread, 0, dz) for dz in range(8)])
+    l_wait(5, 1)
+    l_wait(3, 1)
+    sib_forward(3)
     pltpu.make_async_copy(lmeta.at[pl.ds(8, 8)], lmeta.at[pl.ds(8, 8)], mr_sem.at[0]).wait()
-    for c in range(2):
-        for dz in range(8):
-            m = jnp.broadcast_to(lmeta[8 * c + dz], (128, 128)).T
-            r = LD * lplace(dz, c)
-            lsc[r:r + LD, :] = m[0:LD]
-            lband[r:r + LD, :] = m[64:64 + LD]
-    for n in range(3):
-        l_wait(4, n)
+    multiply(288, 192, 1, [functools.partial(spread, 1, dz) for dz in range(8)])
+    l_wait(4, 0)
     sib_forward(4)
     sib_wait(3)
-    sib_wait(5)
-    multiply(480, 192, 1)
-    select(0, 5, (2, 3))
+    multiply(480, 192, 1, selects(range(3), (2, 3)))
     sib_wait(4)
 
     def finish(t):
@@ -466,14 +466,15 @@
                 recv_sem=f_sem.at[1], device_id=plane(a, b), device_id_type=MESH,
             ).start()
 
-    for h in (1, 0):
-        if h == 0:
-            multiply(480, 192, 0)
-            select(0, 5, (0, 1))
-        multiply(672, 96, h)
-        for t in (2 * h + 1, 2 * h):
-            select(5, 6, (t,))
-            finish(t)
+    multiply(672, 96, 1, selects(range(3, 5), (2, 3)))
+    for t in (3, 2):
+        select(5, t)
+        finish(t)
+    multiply(480, 288, 0, selects(range(3), (0, 1)))
+    for t in (1, 0):
+        for g in range(3, 6):
+            select(g, t)
+        finish(t)
     got[0] = fin[0]
     for c in sends:
         c.wait_send()
@@ -524,8 +525,8 @@
             pltpu.VMEM((16, 1, 128), f32),
             pltpu.VMEM((4, 16, 128), f32),
             pltpu.VMEM((16, 16, 128), f32),
-            dma((5,)), dma((36,)), dma((36,)), dma((21,)), dma((21,)),
-            dma((8,)), dma((8,)), dma((8,)), dma((8,)), dma((2,)),
+            dma((5,)), dma((36,)), dma((37,)), dma((16,)), dma((16,)),
+            dma((5,)), dma((5,)), dma((8,)), dma((8,)), dma((2,)),
         ],
         compiler_params=pltpu.CompilerParams(
             collective_id=0, has_side_effects=True, vmem_limit_bytes=62 * 2**20

time: 43.8 us -> 42 us (0.959)
  Pallas kernels: 42.3 us -> 40.6 us
    pallas_call x1, Pallas kernels: 42.3 us -> 40.6 us  [local(): pl.pallas_call(kernel, out_shape=jax.ShapeDtypeStruct((TOPK, QD), f32), i...]
where the time goes in v4:
time: 42 us; the launch traced here: 41.9 us
  Pallas kernels  40.6 us (97%)
  local copies, waits for them, and re-layouts  1.3 us (3%)
    pallas_call x1, Pallas kernels, local(): pl.pallas_call(kernel, out_shape=jax.ShapeDtypeStruct((TOPK, QD), f32), i...  40.6 us
    unnamed x1, local copies, waits for them, and re-layouts  1.3 us

profile of v4, /device:TPU:1, one launch (start us, length us, event | category | flops | bytes accessed | tf_op | source)
XLA Modules:
  0.0 41.9 jit_solution(12207429727097570307)
XLA Ops:
  0.0 40.6 %shard_map.55 = f32[16,32]{1,0:T(8,128)} custom-call(bf16[32,2048]{1,0:T(8,128)(2,1)} %q_in.1, s32[2]{0:T(128)} %w_hbm.1, bf16[48,2048]{1,0:T(8,128)(2,1)} %l_in.1, s32[6]{0:T(128)} %b_hbm.1, s32[4]{0:T(128)} %s_hbm.1), custom_call_target="tpu_custom_call" | custom-call | flops 6442450944 | bytes 327680 | tf_op jit(solution)/shard_map/pallas_call | solution.py:507
  40.6 1.3 %copy.7 = f32[32,16]{0,1:T(8,128)} copy(f32[32,16]{0,1:T(8,128)} %bitcast.1) | data formatting | bytes 4096

commit v5 on v4

--- a/solution.py
+++ b/solution.py
@@ -86,7 +86,7 @@
 def kernel(
     q_in, w_hbm, l_in, b_hbm, s_hbm, out,
     w_in, b_in, s_in, qbuf, lbuf, qt32, qtk, sc, lsc, lband, qrow, best, lmeta, fin, got,
-    loc_sem, qs_sem, qr_sem, ls_sem, lr_sem, ss_sem, sr_sem, ms_sem, mr_sem, f_sem,
+    loc_sem, left_sem, qr_sem, lr_sem, sr_sem, mr_sem, f_sem,
 ):
     blk = lax.axis_index("blk")
     grp = lax.axis_index("grp")
@@ -126,7 +126,8 @@
         c.start()
     pl.semaphore_wait(barrier, len(near))
 
-    sends = []
+    def wait_all(ref, sem):
+        pltpu.make_async_copy(ref, ref, sem).wait()
 
     UP = ((0, 32), (32, 16))
     DOWN = ((16, 32), (0, 16))
@@ -137,53 +138,46 @@
         r, n = (UP if dz > 4 else DOWN)[part]
         return lbuf.at[pl.ds(LD * lplace(dz, 0) + r, n)]
 
-    def l_copy(src, dst, n_send, n_recv, step):
+    def l_copy(src, dst, n, step):
         c = pltpu.make_async_remote_copy(
-            src_ref=src, dst_ref=dst, send_sem=ls_sem.at[n_send],
-            recv_sem=lr_sem.at[n_recv], device_id=column(step, 0), device_id_type=MESH,
+            src_ref=src, dst_ref=dst, send_sem=left_sem.at[0],
+            recv_sem=lr_sem.at[n], device_id=column(step, 0), device_id_type=MESH,
         )
         c.start()
-        sends.append(c)
 
     def l_send(src, dz, part, step):
-        n = 2 * dz + part
-        l_copy(src, lrows(dz, part), n, n, step)
-
-    def l_wait(dz, part):
-        ref = lrows(dz, part)
-        pltpu.make_async_copy(ref, ref, lr_sem.at[2 * dz + part]).wait()
+        l_copy(src, lrows(dz, part), 2 * min(dz, 8 - dz) + part, step)
+
+    def l_wait(d, part):
+        wait_all(lbuf.at[pl.ds(0, LD if d == 4 else (64, 32)[part])], lr_sem.at[2 * d + part])
 
     def l_forward(d, part):
-        l_wait(8 - d, part)
         l_wait(d, part)
         l_send(lrows(8 - d, part), 7 - d, part, 1)
         l_send(lrows(d, part), d + 1, part, 7)
 
     def l_last():
-        l_wait(5, 0)
         l_wait(3, 0)
         up, down, far = (LD * lplace(dz, 0) for dz in (5, 3, 4))
         mid = up * (1 - core) + down * core + CH
-        for i, (src, r, step) in enumerate(
-            ((up, 0, 1), (down + 2 * CH, 2 * CH, 7), (mid, CH, 1 + 6 * core))
+        for src, r, step in (
+            (up, 0, 1), (down + 2 * CH, 2 * CH, 7), (mid, CH, 1 + 6 * core)
         ):
             src = lbuf.at[pl.ds(pl.multiple_of(src, CH), CH)]
-            l_copy(src, lbuf.at[pl.ds(far + r, CH)], (8, 9, 0)[i], 8, step)
+            l_copy(src, lbuf.at[pl.ds(far + r, CH)], 8, step)
 
     def m_send(src_dz, dst_dz, step):
         c = pltpu.make_async_remote_copy(
             src_ref=lmeta.at[src_dz], dst_ref=lmeta.at[dst_dz],
-            send_sem=ms_sem.at[dst_dz], recv_sem=mr_sem.at[dst_dz],
+            send_sem=left_sem.at[1], recv_sem=mr_sem.at[min(dst_dz, 8 - dst_dz)],
             device_id=column(step, 0), device_id_type=MESH,
         )
         c.start()
-        sends.append(c)
-
-    def m_wait(dz):
-        pltpu.make_async_copy(lmeta.at[dz], lmeta.at[dz], mr_sem.at[dz]).wait()
+
+    def m_wait(d):
+        wait_all(lmeta.at[pl.ds(0, 1 if d == 4 else 2)], mr_sem.at[d])
 
     def m_forward(d):
-        m_wait(8 - d)
         m_wait(d)
         m_send(8 - d, 7 - d, 1)
         if d < 3:
@@ -193,11 +187,10 @@
         rows = src.shape[0]
         c = pltpu.make_async_remote_copy(
             src_ref=src, dst_ref=lbuf.at[pl.ds(LD * lplace(d, 1), rows)],
-            send_sem=ss_sem.at[d], recv_sem=sr_sem.at[d],
+            send_sem=left_sem.at[2], recv_sem=sr_sem.at[d],
             device_id=column(0, 1), device_id_type=MESH,
         )
         c.start()
-        sends.append(c)
 
     def sib_forward(d):
         sib(lbuf.at[pl.ds(LD * lplace(d, 0), LD if d == 4 else 2 * LD)], d)
@@ -212,19 +205,18 @@
     def is_last(a, b, half):
         return b == 2 or (a, b, half) in ((3, 1, 0), (3, 3, 1), (2, 1, 0), (2, 3, 1))
 
-    def q_copy(src, dst, n, to, last=False):
+    def q_copy(src, dst, n, to, kind, last=False):
         c = pltpu.make_async_remote_copy(
-            src_ref=src, dst_ref=dst, send_sem=qs_sem.at[n],
+            src_ref=src, dst_ref=dst, send_sem=left_sem.at[kind],
             recv_sem=qr_sem.at[36 if last else n], device_id=plane(to[0] % 4, to[1] % 4),
             device_id_type=MESH,
         )
         c.start()
-        sends.append(c)
 
     def q_own(a, b, to):
         for half in range(2):
             dst = qbuf.at[pl.ds(QD * qslot(a, b) + 16 * half, 16), pl.ds(0, BINS)]
-            q_copy(q_in.at[pl.ds(16 * half, 16)], dst, qslot(a, b) * 2 + half, to)
+            q_copy(q_in.at[pl.ds(16 * half, 16)], dst, qslot(a, b) * 2 + half, to, 3)
 
     EXT = ((1, 0), (3, 0), (0, 1), (0, 3))
 
@@ -232,7 +224,7 @@
         return qbuf.at[pl.ds(QD * qslot(a, b), QD), pl.ds(BINS, 128)]
 
     def q_ext(a, b, to):
-        q_copy(ext_ref(0, 0), ext_ref(a, b), 32 + EXT.index((a, b)), to)
+        q_copy(ext_ref(0, 0), ext_ref(a, b), 32 + EXT.index((a, b)), to, 4)
 
     def ext_wait(a, b):
         ref = ext_ref(a, b)
@@ -241,7 +233,7 @@
     def q_send(a, b, half, to):
         na, nb = (a - to[0]) % 4, (b - to[1]) % 4
         n = qslot(na, nb) * 2 + half
-        q_copy(qrows(a, b, half), qrows(na, nb, half), n, to, is_last(na, nb, half))
+        q_copy(qrows(a, b, half), qrows(na, nb, half), n, to, 5, is_last(na, nb, half))
 
     def q_wait(a, b, half):
         rows = pl.ds(QD * qslot(a, b) + 16 * half, 16)
@@ -304,20 +296,21 @@
     eye_c = lax.broadcasted_iota(jnp.int32, (256, 256), 1)
     eye = (eye_r == eye_c).astype(jnp.float32).astype(jnp.bfloat16)
 
-    def turned(h, c0, width):
-        return lax.dot_general(
-            eye[0:width, 0:width], qbuf[256 * h:256 * h + 256, c0:c0 + width],
-            (((1,), (1,)), ((), ())), preferred_element_type=jnp.float32,
-        )
-
-    def prepare(h):
-        cols = slice(256 * h, 256 * h + 256)
+    def prepare(tiles):
+        cols = slice(128 * tiles[0], 128 * tiles[-1] + 128)
+
+        def turned(c0, width):
+            return lax.dot_general(
+                eye[0:width, 0:width], qbuf[cols, c0:c0 + width],
+                (((1,), (1,)), ((), ())), preferred_element_type=jnp.float32,
+            )
+
         for c0 in range(0, BINS, 256):
-            v = turned(h, c0, 256)
+            v = turned(c0, 256)
             r0 = MAXSHIFT + c0
-            qt32[2 * h, r0:r0 + 256, :] = v[:, 0:128]
-            qt32[2 * h + 1, r0:r0 + 256, :] = v[:, 128:256]
-        ext = turned(h, BINS, 128)
+            for i, t in enumerate(tiles):
+                qt32[t, r0:r0 + 256, :] = v[:, 128 * i:128 * i + 128]
+        ext = turned(BINS, 128)
         qrow[0:1, cols] = ext[1:2] + ext[2:3] + ext[3:4]
         qrow[1:2, cols] = ext[0:1]
         offs = [s_in[k] + MAXSHIFT for k in range(NOFF)]
@@ -326,7 +319,7 @@
         def _(i):
             r0 = pl.multiple_of(i * 128, 128)
             for k in range(NOFF):
-                for t in (2 * h, 2 * h + 1):
+                for t in tiles:
                     v = qt32[t, pl.ds(r0 + offs[k], 128), :]
                     qtk[k, pl.ds(r0, 128), 128 * t:128 * t + 128] = v.astype(jnp.bfloat16)
 
@@ -413,11 +406,12 @@
     q_second(1, 0)
     q_across(1)
     q_second(1, 1)
+    prepare((0,))
     m_forward(2)
     l_forward(2, 0)
     q_rest(0)
     q_rest(1)
-    prepare(0)
+    prepare((1,))
     q_second(3, 1)
     l_forward(2, 1)
     q_second(2, 0)
@@ -432,14 +426,13 @@
     l_last()
     ref = qbuf.at[pl.ds(0, 192)]
     pltpu.make_async_copy(ref, ref, qr_sem.at[36]).wait()
-    prepare(1)
+    prepare((2, 3))
     m_wait(4)
     pltpu.make_async_remote_copy(
-        src_ref=lmeta.at[pl.ds(0, 8)], dst_ref=lmeta.at[pl.ds(8, 8)], send_sem=ms_sem.at[0],
+        src_ref=lmeta.at[pl.ds(0, 8)], dst_ref=lmeta.at[pl.ds(8, 8)], send_sem=left_sem.at[6],
         recv_sem=mr_sem.at[0], device_id=column(0, 1), device_id_type=MESH,
     ).start()
     multiply(0, 288, 1, [functools.partial(spread, 0, dz) for dz in range(8)])
-    l_wait(5, 1)
     l_wait(3, 1)
     sib_forward(3)
     pltpu.make_async_copy(lmeta.at[pl.ds(8, 8)], lmeta.at[pl.ds(8, 8)], mr_sem.at[0]).wait()
@@ -476,9 +469,13 @@
             select(g, t)
         finish(t)
     got[0] = fin[0]
-    for c in sends:
-        c.wait_send()
-    pltpu.make_async_copy(lmeta.at[pl.ds(0, 8)], lmeta.at[pl.ds(0, 8)], ms_sem.at[0]).wait()
+    wait_all(lbuf.at[pl.ds(0, 7 * LD)], left_sem.at[0])
+    wait_all(lmeta.at[pl.ds(0, 7)], left_sem.at[1])
+    wait_all(lbuf.at[pl.ds(0, 8 * LD)], left_sem.at[2])
+    wait_all(lbuf.at[pl.ds(0, 4 * QD)], left_sem.at[3])
+    wait_all(qbuf.at[pl.ds(0, 4 * QD), pl.ds(BINS, 128)], left_sem.at[4])
+    wait_all(qbuf.at[pl.ds(0, 11 * QD)], left_sem.at[5])
+    wait_all(lmeta.at[pl.ds(0, 8)], left_sem.at[6])
     pltpu.make_async_copy(got.at[pl.ds(1, 15)], got.at[pl.ds(1, 15)], f_sem.at[0]).wait()
     pltpu.make_async_copy(got.at[pl.ds(1, 15)], got.at[pl.ds(1, 15)], f_sem.at[1]).wait()
 
@@ -525,8 +522,7 @@
             pltpu.VMEM((16, 1, 128), f32),
             pltpu.VMEM((4, 16, 128), f32),
             pltpu.VMEM((16, 16, 128), f32),
-            dma((5,)), dma((36,)), dma((37,)), dma((16,)), dma((16,)),
-            dma((5,)), dma((5,)), dma((8,)), dma((8,)), dma((2,)),
+            dma((5,)), dma((7,)), dma((37,)), dma((9,)), dma((5,)), dma((5,)), dma((2,)),
         ],
         compiler_params=pltpu.CompilerParams(
             collective_id=0, has_side_effects=True, vmem_limit_bytes=62 * 2**20

time: 42 us -> 42.6 us (1.014)
  Pallas kernels: 40.6 us -> 41.1 us
    pallas_call x1, Pallas kernels: 40.6 us -> 41.1 us  [local(): pl.pallas_call(kernel, out_shape=jax.ShapeDtypeStruct((TOPK, QD), f32), i...]
where the time goes in v5:
time: 42.6 us; the launch traced here: 42.4 us
  Pallas kernels  41.1 us (96%)
  local copies, waits for them, and re-layouts  1.3 us (3%)
    pallas_call x1, Pallas kernels, local(): pl.pallas_call(kernel, out_shape=jax.ShapeDtypeStruct((TOPK, QD), f32), i...  41.1 us
    unnamed x1, local copies, waits for them, and re-layouts  1.3 us

profile of v5, /device:TPU:1, one launch (start us, length us, event | category | flops | bytes accessed | tf_op | source)
XLA Modules:
  0.0 42.4 jit_solution(422192630091943026)
XLA Ops:
  0.0 41.1 %shard_map.55 = f32[16,32]{1,0:T(8,128)} custom-call(bf16[32,2048]{1,0:T(8,128)(2,1)} %q_in.1, s32[2]{0:T(128)} %w_hbm.1, bf16[48,2048]{1,0:T(8,128)(2,1)} %l_in.1, s32[6]{0:T(128)} %b_hbm.1, s32[4]{0:T(128)} %s_hbm.1), custom_call_target="tpu_custom_call" | custom-call | flops 6442450944 | bytes 327680 | tf_op jit(solution)/shard_map/pallas_call | solution.py:504
  41.1 1.3 %copy.7 = f32[32,16]{0,1:T(8,128)} copy(f32[32,16]{0,1:T(8,128)} %bitcast.1) | data formatting | bytes 4096

commit v6 on v5

--- a/solution.py
+++ b/solution.py
@@ -421,9 +421,9 @@
     sib_wait(0)
     sib_wait(1)
     multiply(0, 288, 0)
+    l_last()
     sib_wait(2)
     multiply(288, 192, 0)
-    l_last()
     ref = qbuf.at[pl.ds(0, 192)]
     pltpu.make_async_copy(ref, ref, qr_sem.at[36]).wait()
     prepare((2, 3))
@@ -435,12 +435,11 @@
     multiply(0, 288, 1, [functools.partial(spread, 0, dz) for dz in range(8)])
     l_wait(3, 1)
     sib_forward(3)
+    l_wait(4, 0)
+    sib_forward(4)
     pltpu.make_async_copy(lmeta.at[pl.ds(8, 8)], lmeta.at[pl.ds(8, 8)], mr_sem.at[0]).wait()
     multiply(288, 192, 1, [functools.partial(spread, 1, dz) for dz in range(8)])
-    l_wait(4, 0)
-    sib_forward(4)
     sib_wait(3)
-    multiply(480, 192, 1, selects(range(3), (2, 3)))
     sib_wait(4)
 
     def finish(t):
@@ -459,15 +458,12 @@
                 recv_sem=f_sem.at[1], device_id=plane(a, b), device_id_type=MESH,
             ).start()
 
-    multiply(672, 96, 1, selects(range(3, 5), (2, 3)))
-    for t in (3, 2):
-        select(5, t)
-        finish(t)
-    multiply(480, 288, 0, selects(range(3), (0, 1)))
-    for t in (1, 0):
-        for g in range(3, 6):
-            select(g, t)
-        finish(t)
+    for tiles in ((3, 2), (1, 0)):
+        multiply(480, 288, tiles[1] // 2, selects(range(3), tiles))
+        for t in tiles:
+            for g in range(3, 6):
+                select(g, t)
+            finish(t)
     got[0] = fin[0]
     wait_all(lbuf.at[pl.ds(0, 7 * LD)], left_sem.at[0])
     wait_all(lmeta.at[pl.ds(0, 7)], left_sem.at[1])

time: 42.6 us -> 42.2 us (level)
  no operation moved by 1% of the time
where the time goes in v6:
time: 42.2 us; the launch traced here: 42.1 us
  Pallas kernels  40.8 us (97%)
  local copies, waits for them, and re-layouts  1.3 us (3%)
    pallas_call x1, Pallas kernels, local(): pl.pallas_call(kernel, out_shape=jax.ShapeDtypeStruct((TOPK, QD), f32), i...  40.8 us
    unnamed x1, local copies, waits for them, and re-layouts  1.3 us

profile of v6, /device:TPU:1, one launch (start us, length us, event | category | flops | bytes accessed | tf_op | source)
XLA Modules:
  0.0 42.1 jit_solution(10666253338534226586)
XLA Ops:
  0.0 40.8 %shard_map.55 = f32[16,32]{1,0:T(8,128)} custom-call(bf16[32,2048]{1,0:T(8,128)(2,1)} %q_in.1, s32[2]{0:T(128)} %w_hbm.1, bf16[48,2048]{1,0:T(8,128)(2,1)} %l_in.1, s32[6]{0:T(128)} %b_hbm.1, s32[4]{0:T(128)} %s_hbm.1), custom_call_target="tpu_custom_call" | custom-call | flops 6442450944 | bytes 327680 | tf_op jit(solution)/shard_map/pallas_call | solution.py:500
  40.8 1.3 %copy.7 = f32[32,16]{0,1:T(8,128)} copy(f32[32,16]{0,1:T(8,128)} %bitcast.1) | data formatting | bytes 4096

commit v7 on v6

--- a/solution.py
+++ b/solution.py
@@ -202,13 +202,17 @@
     def qrows(a, b, half):
         return qbuf.at[pl.ds(QD * qslot(a, b) + 16 * half, 16)]
 
-    def is_last(a, b, half):
-        return b == 2 or (a, b, half) in ((3, 1, 0), (3, 3, 1), (2, 1, 0), (2, 3, 1))
-
-    def q_copy(src, dst, n, to, kind, last=False):
+    def arrival(a, b, half):
+        if b == 2:
+            return 36
+        if (a, b, half) in ((3, 1, 0), (3, 3, 1), (2, 1, 0), (2, 3, 1)):
+            return 37
+        return qslot(a, b) * 2 + half
+
+    def q_copy(src, dst, n, to, kind):
         c = pltpu.make_async_remote_copy(
             src_ref=src, dst_ref=dst, send_sem=left_sem.at[kind],
-            recv_sem=qr_sem.at[36 if last else n], device_id=plane(to[0] % 4, to[1] % 4),
+            recv_sem=qr_sem.at[n], device_id=plane(to[0] % 4, to[1] % 4),
             device_id_type=MESH,
         )
         c.start()
@@ -232,8 +236,7 @@
 
     def q_send(a, b, half, to):
         na, nb = (a - to[0]) % 4, (b - to[1]) % 4
-        n = qslot(na, nb) * 2 + half
-        q_copy(qrows(a, b, half), qrows(na, nb, half), n, to, 5, is_last(na, nb, half))
+        q_copy(qrows(a, b, half), qrows(na, nb, half), arrival(na, nb, half), to, 5)
 
     def q_wait(a, b, half):
         rows = pl.ds(QD * qslot(a, b) + 16 * half, 16)
@@ -424,9 +427,10 @@
     l_last()
     sib_wait(2)
     multiply(288, 192, 0)
-    ref = qbuf.at[pl.ds(0, 192)]
-    pltpu.make_async_copy(ref, ref, qr_sem.at[36]).wait()
-    prepare((2, 3))
+    wait_all(qbuf.at[pl.ds(0, 64)], qr_sem.at[37])
+    prepare((2,))
+    wait_all(qbuf.at[pl.ds(0, 128)], qr_sem.at[36])
+    prepare((3,))
     m_wait(4)
     pltpu.make_async_remote_copy(
         src_ref=lmeta.at[pl.ds(0, 8)], dst_ref=lmeta.at[pl.ds(8, 8)], send_sem=left_sem.at[6],
@@ -518,7 +522,7 @@
             pltpu.VMEM((16, 1, 128), f32),
             pltpu.VMEM((4, 16, 128), f32),
             pltpu.VMEM((16, 16, 128), f32),
-            dma((5,)), dma((7,)), dma((37,)), dma((9,)), dma((5,)), dma((5,)), dma((2,)),
+            dma((5,)), dma((7,)), dma((38,)), dma((9,)), dma((5,)), dma((5,)), dma((2,)),
         ],
         compiler_params=pltpu.CompilerParams(
             collective_id=0, has_side_effects=True, vmem_limit_bytes=62 * 2**20

time: 42.2 us -> 41.8 us (level)
  no operation moved by 1% of the time
where the time goes in v7:
time: 41.8 us; the launch traced here: 41.7 us
  Pallas kernels  40.4 us (97%)
  local copies, waits for them, and re-layouts  1.3 us (3%)
    pallas_call x1, Pallas kernels, local(): pl.pallas_call(kernel, out_shape=jax.ShapeDtypeStruct((TOPK, QD), f32), i...  40.4 us
    unnamed x1, local copies, waits for them, and re-layouts  1.3 us

profile of v7, /device:TPU:1, one launch (start us, length us, event | category | flops | bytes accessed | tf_op | source)
XLA Modules:
  0.0 41.7 jit_solution(1605890270641837885)
XLA Ops:
  0.0 40.4 %shard_map.55 = f32[16,32]{1,0:T(8,128)} custom-call(bf16[32,2048]{1,0:T(8,128)(2,1)} %q_in.1, s32[2]{0:T(128)} %w_hbm.1, bf16[48,2048]{1,0:T(8,128)(2,1)} %l_in.1, s32[6]{0:T(128)} %b_hbm.1, s32[4]{0:T(128)} %s_hbm.1), custom_call_target="tpu_custom_call" | custom-call | flops 6442450944 | bytes 327680 | tf_op jit(solution)/shard_map/pallas_call | solution.py:504
  40.4 1.3 %copy.7 = f32[32,16]{0,1:T(8,128)} copy(f32[32,16]{0,1:T(8,128)} %bitcast.1) | data formatting | bytes 4096
